TPU v7x, 32 devices: a whole 2x2x4 slice. The times are simulated.
32 devices in a mesh: sweep: 2 (over x), tp: 8 (over z, y), pp: 2 (over core).
Axes of the slice: x: 2, y: 2, z: 4, core: 2. Of those that a mesh axis runs over, the one named last changes fastest.
Arguments:
- tokens: bfloat16 [256, 8192], P(None, 'tp')
- cotangent: bfloat16 [256, 8192], P(None, 'tp'), may hold values from -6 to 6
- norm_gain: bfloat16 [4, 8192], P(('sweep', 'pp'), 'tp'), parts along dimension 0, may hold values from 0.099609375 to 1.8984375
- gate_band: bfloat16 [4, 64, 2048, 256], P(('sweep', 'pp'), 'tp'), parts along dimension 0, may hold values from -0.125 to 0.125
- up_band: bfloat16 [4, 64, 2048, 256], P(('sweep', 'pp'), 'tp'), parts along dimension 0, may hold values from -0.125 to 0.125
- down_band: bfloat16 [4, 64, 256, 2048], P(('sweep', 'pp'), 'tp'), parts along dimension 0, may hold values from -0.09375 to 0.09375
- offsets: int32 [4, 64], P(('sweep', 'pp'), 'tp'), parts along dimension 0, may hold values from 0 to 31, as said below
- counts: int32 [4], P('sweep'), parts along dimension 0, may hold values from 32 to 128, as said below
Outputs:
- layer_outputs: bfloat16 [4, 256, 8192], P(('sweep', 'pp'), None, 'tp'), parts along dimension 0
- input_grads: bfloat16 [4, 256, 8192], P(('sweep', 'pp'), None, 'tp'), parts along dimension 0
- gate_grads: bfloat16 [4, 64, 2048, 256], P(('sweep', 'pp'), 'tp'), parts along dimension 0
- up_grads: bfloat16 [4, 64, 2048, 256], P(('sweep', 'pp'), 'tp'), parts along dimension 0
- down_grads: bfloat16 [4, 64, 256, 2048], P(('sweep', 'pp'), 'tp'), parts along dimension 0
There are 2 independent parts, one for each index of `sweep`. A program takes and returns all parts, laid end to end along the dimension named above; an argument that names none is the same for every part. Nothing has to cross between parts.
Inputs may be any that keep to these rules, and one draw needn't show every extreme that they name: offsets[l, h] = (h * 8192 // 16384 - 8 // 2 + b) mod (32) with b equal to 0 or 1 for each (l, h). `counts`: the valid tokens of a micro-batch are its first ones; some micro-batch is full.
All inputs are finite; a program needn't handle non-finite values.
Results may differ from a plain program's by a relative error of at most 0.0084.
Values may be sent and summed in bfloat16 or wider, within the bound.
A program may use at most 448 MiB of HBM per device.

v0:
```python
import jax
import jax.numpy as jnp
from jax import lax
from jax.sharding import PartitionSpec as P

D = 8192
BLK = 256
T_MB = 128
MICRO = 2
KB = 8
BAND = 2048


EPSILON = 1e-05


def from_behind(value, axis, by):
    length = lax.axis_size(axis)
    return lax.ppermute(value, axis, [(i, (i + by) % length) for i in range(length)])


def from_behind_2(value, axis, steps):
    count = lax.axis_size(axis)
    initial, last = (max(0, -steps), min(count, count - steps))
    return lax.ppermute(value, axis, [(source, source + steps) for source in range(initial, last)])


def band_window(shard_block, reach_devs):
    lower_list = []
    upper_list = []
    for stride in range(1, reach_devs + 1):
        lower_list.append(from_behind(shard_block, "tp", stride))
        upper_list.append(from_behind(shard_block, "tp", -stride))
    return jnp.concatenate(lower_list[::-1] + [shard_block] + upper_list, axis=1)


def band_sum(partial_sums, reach_devs, shard_width):

    def portion(offset):
        return partial_sums[
            :, (reach_devs + offset) * shard_width : (reach_devs + offset + 1) * shard_width
        ]

    combined = portion(0)
    for stride in range(1, reach_devs + 1):
        combined = combined + from_behind(portion(stride), "tp", stride)
        combined = combined + from_behind(portion(-stride), "tp", -stride)
    return combined


def shards(tokens, cotangent, norm_gain, gate_band, up_band, down_band, offsets, counts):
    shard_width = tokens.shape[1]
    blocks_dev = shard_width // BLK
    reach_devs = (KB // 2 - 1 + blocks_dev) // blocks_dev
    window_width = (2 * reach_devs + 1) * shard_width
    hidden_blocks = offsets.shape[1]
    section_index = lax.axis_index("pp")
    sections = lax.axis_size("pp")
    position = lax.axis_index("tp")
    starts = jnp.mod(offsets[0] - (position - reach_devs) * blocks_dev, D // BLK) * BLK
    band_index = starts[:, None] + jnp.arange(BAND, dtype=jnp.int32)[None, :]
    flat_index = band_index.reshape(-1)
    gain_row = norm_gain[0].astype(jnp.float32)[None, :]
    gate_up_weight = jnp.concatenate([gate_band[0], up_band[0]], axis=2)
    down_weight = down_band[0]
    tick_count = MICRO + sections - 1

    def take_band(window):
        return jnp.take(window, flat_index, axis=1).reshape(window.shape[0], hidden_blocks, BAND)

    def spread_band(terms):
        rows = terms.shape[0]
        flat_terms = terms.reshape(rows, hidden_blocks * BAND)
        return jnp.zeros((rows, window_width), jnp.float32).at[:, flat_index].add(flat_terms)

    def layer_forward(layer_in):
        rows = layer_in.shape[0]
        act_f32 = layer_in.astype(jnp.float32)
        square_sum = lax.psum(jnp.sum(act_f32 * act_f32, axis=1), "tp")
        inverse = lax.rsqrt(square_sum / D + EPSILON)[:, None]
        normed = (act_f32 * inverse * gain_row).astype(jnp.bfloat16)
        window = band_window(normed, reach_devs)
        gate_up = jnp.einsum(
            "thi,hij->thj", take_band(window), gate_up_weight, preferred_element_type=jnp.float32
        )
        hidden = (jax.nn.silu(gate_up[:, :, :BLK]) * gate_up[:, :, BLK:]).astype(jnp.bfloat16)
        terms = jnp.einsum("thj,hji->thi", hidden, down_weight, preferred_element_type=jnp.float32)
        partial_value = spread_band(terms)
        layer_out = (act_f32 + band_sum(partial_value, reach_devs, shard_width)).astype(
            jnp.bfloat16
        )
        return (layer_out, inverse, window, gate_up)

    def layer_backward(grad_out, layer_in, inverse, window, gate_up):
        rows = grad_out.shape[0]
        grad_window = band_window(grad_out, reach_devs)
        gate_pre = gate_up[:, :, :BLK]
        up_pre = gate_up[:, :, BLK:]
        hidden = (jax.nn.silu(gate_pre) * up_pre).astype(jnp.bfloat16)
        grad_band = take_band(grad_window)
        grad_hidden = jnp.einsum(
            "thi,hji->thj", grad_band, down_weight, preferred_element_type=jnp.float32
        )
        down_parts = jnp.einsum(
            "thj,thi->hji", hidden, grad_band, preferred_element_type=jnp.float32
        )
        sigmoid_gate = jax.nn.sigmoid(gate_pre)
        grad_gate = (
            grad_hidden * up_pre * sigmoid_gate * (1.0 + gate_pre * (1.0 - sigmoid_gate))
        ).astype(jnp.bfloat16)
        grad_up = (grad_hidden * (gate_pre * sigmoid_gate)).astype(jnp.bfloat16)
        both_grads = jnp.concatenate([grad_gate, grad_up], axis=2)
        weight_parts = jnp.einsum(
            "thi,thj->hij", take_band(window), both_grads, preferred_element_type=jnp.float32
        )
        terms = jnp.einsum(
            "thj,hij->thi", both_grads, gate_up_weight, preferred_element_type=jnp.float32
        )
        partial_value = spread_band(terms)
        grad_normed = band_sum(partial_value, reach_devs, shard_width)
        act_f32 = layer_in.astype(jnp.float32)
        normed_f32 = act_f32 * inverse
        scaled = grad_normed * gain_row
        projection = lax.psum(jnp.sum(scaled * normed_f32, axis=1), "tp") / D
        grad_in = (
            grad_out.astype(jnp.float32) + inverse * (scaled - normed_f32 * projection[:, None])
        ).astype(jnp.bfloat16)
        return (grad_in, weight_parts[:, :, :BLK], weight_parts[:, :, BLK:], down_parts)

    empty_rows = jnp.zeros((T_MB, shard_width), jnp.bfloat16)
    padding = jnp.zeros(((sections - 1) * T_MB, shard_width), jnp.bfloat16)
    token_ticks = jnp.concatenate([tokens, padding], axis=0).reshape(tick_count, T_MB, shard_width)

    def forward_tick(carried, fresh_rows):
        layer_in = jnp.where(section_index == 0, fresh_rows, carried)
        layer_out, inverse, window, gate_up = layer_forward(layer_in)
        passed = from_behind_2(layer_out, "pp", 1)
        return (passed, (layer_in, layer_out, inverse, window, gate_up))

    unused, stacked = lax.scan(forward_tick, empty_rows, token_ticks)
    layer_outputs = lax.dynamic_slice_in_dim(stacked[1], section_index, MICRO, 0).reshape(
        MICRO * T_MB, shard_width
    )
    cot_ticks = jnp.concatenate([cotangent, padding], axis=0).reshape(tick_count, T_MB, shard_width)
    count_ticks = jnp.concatenate([counts, jnp.zeros((sections - 1,), jnp.int32)], axis=0)
    tick_ids = jnp.arange(tick_count, dtype=jnp.int32)
    row_ids = jnp.arange(T_MB, dtype=jnp.int32)

    def backward_tick(state, inputs):
        grad_carried, gate_total, up_total, down_total = state
        cot_rows, count_now, tick_now = inputs
        valid_rows = row_ids < count_now
        fresh_grad = jnp.where(valid_rows[:, None], cot_rows, jnp.zeros((), jnp.bfloat16))
        grad_out = jnp.where(section_index == sections - 1, fresh_grad, grad_carried)
        micro_id = tick_now - (sections - 1 - section_index)
        weight_on = ((micro_id >= 0) & (micro_id < MICRO)).astype(jnp.float32)
        forward_index = jnp.clip(micro_id + section_index, 0, tick_count - 1)
        saved_in = lax.dynamic_index_in_dim(stacked[0], forward_index, 0, keepdims=False)
        saved_inverse = lax.dynamic_index_in_dim(stacked[2], forward_index, 0, keepdims=False)
        saved_window = lax.dynamic_index_in_dim(stacked[3], forward_index, 0, keepdims=False)
        saved_gate_up = lax.dynamic_index_in_dim(stacked[4], forward_index, 0, keepdims=False)
        grad_in, gate_parts, up_parts, down_parts = layer_backward(
            grad_out, saved_in, saved_inverse, saved_window, saved_gate_up
        )
        passed = from_behind_2(grad_in, "pp", -1)
        new_state = (
            passed,
            gate_total + weight_on * gate_parts,
            up_total + weight_on * up_parts,
            down_total + weight_on * down_parts,
        )
        return (new_state, grad_in)

    start_state = (
        empty_rows,
        jnp.zeros(gate_band[0].shape, jnp.float32),
        jnp.zeros(up_band[0].shape, jnp.float32),
        jnp.zeros(down_weight.shape, jnp.float32),
    )
    final_state, grad_stack = lax.scan(
        backward_tick, start_state, (cot_ticks, count_ticks, tick_ids)
    )
    input_grads = lax.dynamic_slice_in_dim(
        grad_stack, sections - 1 - section_index, MICRO, 0
    ).reshape(MICRO * T_MB, shard_width)
    return (
        layer_outputs[None],
        input_grads[None],
        final_state[1].astype(jnp.bfloat16)[None],
        final_state[2].astype(jnp.bfloat16)[None],
        final_state[3].astype(jnp.bfloat16)[None],
    )


def solution(mesh):
    return jax.shard_map(
        shards,
        mesh=mesh,
        in_specs=(
            P(None, "tp"),
            P(None, "tp"),
            P(("sweep", "pp"), "tp"),
            P(("sweep", "pp"), "tp", None, None),
            P(("sweep", "pp"), "tp", None, None),
            P(("sweep", "pp"), "tp", None, None),
            P(("sweep", "pp"), "tp"),
            P("sweep"),
        ),
        out_specs=(
            P(("sweep", "pp"), None, "tp"),
            P(("sweep", "pp"), None, "tp"),
            P(("sweep", "pp"), "tp", None, None),
            P(("sweep", "pp"), "tp", None, None),
            P(("sweep", "pp"), "tp", None, None),
        ),
        check_vma=False,
    )
```

profile of v0, /device:TPU:0, one launch (start us, length us, event | category | flops | bytes accessed | tf_op | source)
XLA Modules:
  0.0 1848.0 jit_solution(11151910463488333920)
XLA Ops:
  7.8 13.6 pad_maximum_fusion.5
  23.3 737.6 %while.43 = (s32[]{:T(128)}, bf16[128,1024]{0,1:T(8,128)(2,1)}, bf16[3,128,1024]{1,2,0:T(8,128)(2,1)S(1)}, bf16[3,128,1024]{1,2,0:T(8,128)(2,1)}, f32[3,128,1]{1...) while((s32[]{:T(128)}, bf16[128,1024]{0,1:T(8,128)(2,1)}, ...), condition=%wide.region_4.6_spmd.clone, body=%wide.region_0.5_spmd.clone.sunk | while | flops 3233645056 | bytes 122987456 | solution.py:140
  24.8 23.1 %psum.21 = f32[128]{0:T(128)S(1)} all-reduce(f32[128]{0:T(128)S(1)} %fusion.89), channel_id=1, replica_groups=mesh['sweep'=2,'tp'=8,'pp'=2] {'tp'}, use_global_device_ids=true, to_apply=%region_2.2 | all-reduce | flops 128 | bytes 1024 | tf_op jit(solution)/shard_map/while/body/eval_jaxpr/psum | solution.py:79
  59.1 57.9 %gather_fusion = bf16[16384,128]{1,0:T(8,128)(2,1)} fusion(bf16[128,3072]{0,1:T(8,128)(2,1)S(1)} %pad_maximum_fusion.10, s32[16384]{0:T(1024)S(1)} %fusion.91), kind=kCustom, calls=%fused_computation.clone.clone.1 | custom fusion | bytes 8454144 | tf_op jit(solution)/shard_map/while/body/eval_jaxpr/jit(_take)/gather | solution.py:69
  117.0 10.9 broadcast_select_fusion.5
  128.0 10.6 bitcast_dynamic-update-slice_fusion.11
  154.0 88.0 %scatter_custom_fusion.11 = f32[128,3072]{0,1:T(8,128)S(1)} fusion(s32[16384]{0:T(1024)S(1)} %bitcast.196, f32[16384,128]{1,0:T(8,128)} %bitcast.184, f32[]{:T(128)} %constant.129.clone.3..sunk), kind=kCustom, calls=%fused_computation.15.clone.1 | custom fusion | flops 2097152 | bytes 1573376 | tf_op jit(solution)/shard_map/while/body/eval_jaxpr/scatter-add | solution.py:74
  246.4 19.6 %collective-permute-done.2 = f32[128,1024]{0,1:T(8,128)} collective-permute-done((f32[128,1024]{0,1:T(8,128)}, f32[128,1024]{0,1:T(8,128)}, u32[]{:S(2)}, u32[]{:S(2)}) %collective-permute-start.2) | collective-permute-done | bytes 524320 | tf_op jit(solution)/shard_map/while/body/eval_jaxpr/ppermute | solution.py:19
  272.4 20.0 %psum.21 = f32[128]{0:T(128)S(1)} all-reduce(f32[128]{0:T(128)S(1)} %fusion.89), channel_id=1, replica_groups=mesh['sweep'=2,'tp'=8,'pp'=2] {'tp'}, use_global_device_ids=true, to_apply=%region_2.2 | all-reduce | flops 128 | bytes 1024 | tf_op jit(solution)/shard_map/while/body/eval_jaxpr/psum | solution.py:79
  304.1 57.9 %gather_fusion = bf16[16384,128]{1,0:T(8,128)(2,1)} fusion(bf16[128,3072]{0,1:T(8,128)(2,1)S(1)} %pad_maximum_fusion.10, s32[16384]{0:T(1024)S(1)} %fusion.91), kind=kCustom, calls=%fused_computation.clone.clone.1 | custom fusion | bytes 8454144 | tf_op jit(solution)/shard_map/while/body/eval_jaxpr/jit(_take)/gather | solution.py:69
  362.0 10.9 broadcast_select_fusion.5
  373.0 10.6 bitcast_dynamic-update-slice_fusion.11
  399.0 88.0 %scatter_custom_fusion.11 = f32[128,3072]{0,1:T(8,128)S(1)} fusion(s32[16384]{0:T(1024)S(1)} %bitcast.196, f32[16384,128]{1,0:T(8,128)} %bitcast.184, f32[]{:T(128)} %constant.129.clone.3..sunk), kind=kCustom, calls=%fused_computation.15.clone.1 | custom fusion | flops 2097152 | bytes 1573376 | tf_op jit(solution)/shard_map/while/body/eval_jaxpr/scatter-add | solution.py:74
  491.1 20.2 %collective-permute-done.2 = f32[128,1024]{0,1:T(8,128)} collective-permute-done((f32[128,1024]{0,1:T(8,128)}, f32[128,1024]{0,1:T(8,128)}, u32[]{:S(2)}, u32[]{:S(2)}) %collective-permute-start.2) | collective-permute-done | bytes 524320 | tf_op jit(solution)/shard_map/while/body/eval_jaxpr/ppermute | solution.py:19
  517.7 20.0 %psum.21 = f32[128]{0:T(128)S(1)} all-reduce(f32[128]{0:T(128)S(1)} %fusion.89), channel_id=1, replica_groups=mesh['sweep'=2,'tp'=8,'pp'=2] {'tp'}, use_global_device_ids=true, to_apply=%region_2.2 | all-reduce | flops 128 | bytes 1024 | tf_op jit(solution)/shard_map/while/body/eval_jaxpr/psum | solution.py:79
  549.1 57.9 %gather_fusion = bf16[16384,128]{1,0:T(8,128)(2,1)} fusion(bf16[128,3072]{0,1:T(8,128)(2,1)S(1)} %pad_maximum_fusion.10, s32[16384]{0:T(1024)S(1)} %fusion.91), kind=kCustom, calls=%fused_computation.clone.clone.1 | custom fusion | bytes 8454144 | tf_op jit(solution)/shard_map/while/body/eval_jaxpr/jit(_take)/gather | solution.py:69
  607.0 10.9 broadcast_select_fusion.5
  644.0 88.0 %scatter_custom_fusion.11 = f32[128,3072]{0,1:T(8,128)S(1)} fusion(s32[16384]{0:T(1024)S(1)} %bitcast.196, f32[16384,128]{1,0:T(8,128)} %bitcast.184, f32[]{:T(128)} %constant.129.clone.3..sunk), kind=kCustom, calls=%fused_computation.15.clone.1 | custom fusion | flops 2097152 | bytes 1573376 | tf_op jit(solution)/shard_map/while/body/eval_jaxpr/scatter-add | solution.py:74
  736.4 19.6 %collective-permute-done.2 = f32[128,1024]{0,1:T(8,128)} collective-permute-done((f32[128,1024]{0,1:T(8,128)}, f32[128,1024]{0,1:T(8,128)}, u32[]{:S(2)}, u32[]{:S(2)}) %collective-permute-start.2) | collective-permute-done | bytes 524320 | tf_op jit(solution)/shard_map/while/body/eval_jaxpr/ppermute | solution.py:19
  764.1 1055.9 %while.44 = (s32[]{:T(128)}, bf16[128,1024]{0,1:T(8,128)(2,1)S(1)}, f32[8,2048,256]{2,1,0:T(8,128)}, f32[8,2048,256]{2,1,0:T(8,128)}, f32[8,256,2048]{2,1,0:T(8,...) while((s32[]{:T(128)}, bf16[128,1024]{0,1:T(8,128)(2,1)S(1)}, ...), condition=%wide.region_9.11_spmd.clone, body=%wide.region_5.10_spmd.clone.sunk | while | flops 6500483072 | bytes 332280896 | solution.py:180
  774.2 57.9 %gather_fusion.1 = bf16[16384,128]{1,0:T(8,128)(2,1)} fusion(bf16[128,3072]{0,1:T(8,128)(2,1)S(1)} %dynamic-slice_bitcast_fusion.5, s32[16384]{0:T(1024)S(1)} %fusion.101), kind=kCustom, calls=%fused_computation.2.clone.clone.1 | custom fusion | bytes 8454144 | tf_op jit(solution)/shard_map/while/body/eval_jaxpr/jit(_take)/gather | solution.py:69
  836.3 57.9 %gather_fusion.2 = bf16[16384,128]{1,0:T(8,128)(2,1)} fusion(bf16[128,3072]{0,1:T(8,128)(2,1)S(1)} %pad_maximum_fusion.13, s32[16384]{0:T(1024)S(1)} %fusion.101), kind=kCustom, calls=%fused_computation.1.clone.clone.1 | custom fusion | bytes 8454144 | tf_op jit(solution)/shard_map/while/body/eval_jaxpr/jit(_take)/gather | solution.py:69
  894.2 12.3 broadcast_select_fusion.6
  915.3 15.0 convolution_bitcast_fusion.6
  939.5 88.0 %scatter_custom_fusion.13 = f32[128,3072]{0,1:T(8,128)S(1)} fusion(s32[16384]{0:T(1024)S(1)} %bitcast.195, f32[16384,128]{1,0:T(8,128)} %bitcast.185, f32[]{:T(128)} %constant.129.clone.3..sunk.1), kind=kCustom, calls=%fused_computation.59.clone.1 | custom fusion | flops 2097152 | bytes 1573376 | tf_op jit(solution)/shard_map/while/body/eval_jaxpr/scatter-add | solution.py:74
  1029.7 17.9 fusion.105
  1047.5 21.3 %fusion.106 = (f32[8,2048,256]{2,1,0:T(8,128)}, f32[8,2048,256]{2,1,0:T(8,128)}) fusion(f32[8,2048,512]{2,1,0:T(8,128)} %fusion.105, f32[8,2048,256]{2,1,0:T(8,128)} %get-tuple-element.894, f32[]{:T(128)S(6)} %convert_element_type.121, pred[]{:T(512)S(6)} %compare.9, f32[8,2048,256]{2,1,0:T(8,128)} %get-tuple-element.893), kind=kLoop, calls=%fused_computation.42.clone.1 | loop fusion | flops 25165824 | bytes 100663304 | tf_op jit(solution)/shard_map/while/body/eval_jaxpr/add | solution.py:169
  1070.1 20.2 %psum.22 = f32[128]{0:T(128)S(1)} all-reduce(f32[128]{0:T(128)S(1)} %get-tuple-element.816), channel_id=1, replica_groups=mesh['sweep'=2,'tp'=8,'pp'=2] {'tp'}, use_global_device_ids=true, to_apply=%region_8.9 | all-reduce | flops 128 | bytes 1024 | tf_op jit(solution)/shard_map/while/body/eval_jaxpr/psum | solution.py:124
  1093.4 11.5 select_add_fusion.2
  1115.1 57.9 %gather_fusion.1 = bf16[16384,128]{1,0:T(8,128)(2,1)} fusion(bf16[128,3072]{0,1:T(8,128)(2,1)S(1)} %dynamic-slice_bitcast_fusion.5, s32[16384]{0:T(1024)S(1)} %fusion.101), kind=kCustom, calls=%fused_computation.2.clone.clone.1 | custom fusion | bytes 8454144 | tf_op jit(solution)/shard_map/while/body/eval_jaxpr/jit(_take)/gather | solution.py:69
  1177.2 57.9 %gather_fusion.2 = bf16[16384,128]{1,0:T(8,128)(2,1)} fusion(bf16[128,3072]{0,1:T(8,128)(2,1)S(1)} %pad_maximum_fusion.13, s32[16384]{0:T(1024)S(1)} %fusion.101), kind=kCustom, calls=%fused_computation.1.clone.clone.1 | custom fusion | bytes 8454144 | tf_op jit(solution)/shard_map/while/body/eval_jaxpr/jit(_take)/gather | solution.py:69
  1235.1 12.3 broadcast_select_fusion.6
  1256.2 15.0 convolution_bitcast_fusion.6
  1280.4 88.0 %scatter_custom_fusion.13 = f32[128,3072]{0,1:T(8,128)S(1)} fusion(s32[16384]{0:T(1024)S(1)} %bitcast.195, f32[16384,128]{1,0:T(8,128)} %bitcast.185, f32[]{:T(128)} %constant.129.clone.3..sunk.1), kind=kCustom, calls=%fused_computation.59.clone.1 | custom fusion | flops 2097152 | bytes 1573376 | tf_op jit(solution)/shard_map/while/body/eval_jaxpr/scatter-add | solution.py:74
  1370.5 17.9 fusion.105
  1388.4 33.4 %fusion.106 = (f32[8,2048,256]{2,1,0:T(8,128)}, f32[8,2048,256]{2,1,0:T(8,128)}) fusion(f32[8,2048,512]{2,1,0:T(8,128)} %fusion.105, f32[8,2048,256]{2,1,0:T(8,128)} %get-tuple-element.894, f32[]{:T(128)S(6)} %convert_element_type.121, pred[]{:T(512)S(6)} %compare.9, f32[8,2048,256]{2,1,0:T(8,128)} %get-tuple-element.893), kind=kLoop, calls=%fused_computation.42.clone.1 | loop fusion | flops 25165824 | bytes 100663304 | tf_op jit(solution)/shard_map/while/body/eval_jaxpr/add | solution.py:169
  1423.0 19.9 %psum.22 = f32[128]{0:T(128)S(1)} all-reduce(f32[128]{0:T(128)S(1)} %get-tuple-element.816), channel_id=1, replica_groups=mesh['sweep'=2,'tp'=8,'pp'=2] {'tp'}, use_global_device_ids=true, to_apply=%region_8.9 | all-reduce | flops 128 | bytes 1024 | tf_op jit(solution)/shard_map/while/body/eval_jaxpr/psum | solution.py:124
  1446.0 16.3 select_add_fusion.2
  1472.6 57.9 %gather_fusion.1 = bf16[16384,128]{1,0:T(8,128)(2,1)} fusion(bf16[128,3072]{0,1:T(8,128)(2,1)S(1)} %dynamic-slice_bitcast_fusion.5, s32[16384]{0:T(1024)S(1)} %fusion.101), kind=kCustom, calls=%fused_computation.2.clone.clone.1 | custom fusion | bytes 8454144 | tf_op jit(solution)/shard_map/while/body/eval_jaxpr/jit(_take)/gather | solution.py:69
  1534.8 57.9 %gather_fusion.2 = bf16[16384,128]{1,0:T(8,128)(2,1)} fusion(bf16[128,3072]{0,1:T(8,128)(2,1)S(1)} %pad_maximum_fusion.13, s32[16384]{0:T(1024)S(1)} %fusion.101), kind=kCustom, calls=%fused_computation.1.clone.clone.1 | custom fusion | bytes 8454144 | tf_op jit(solution)/shard_map/while/body/eval_jaxpr/jit(_take)/gather | solution.py:69
  1592.6 12.3 broadcast_select_fusion.6
  1613.8 15.0 convolution_bitcast_fusion.6
  1637.9 88.0 %scatter_custom_fusion.13 = f32[128,3072]{0,1:T(8,128)S(1)} fusion(s32[16384]{0:T(1024)S(1)} %bitcast.195, f32[16384,128]{1,0:T(8,128)} %bitcast.185, f32[]{:T(128)} %constant.129.clone.3..sunk.1), kind=kCustom, calls=%fused_computation.59.clone.1 | custom fusion | flops 2097152 | bytes 1573376 | tf_op jit(solution)/shard_map/while/body/eval_jaxpr/scatter-add | solution.py:74
  1728.1 17.9 fusion.105
  1746.0 33.4 %fusion.106 = (f32[8,2048,256]{2,1,0:T(8,128)}, f32[8,2048,256]{2,1,0:T(8,128)}) fusion(f32[8,2048,512]{2,1,0:T(8,128)} %fusion.105, f32[8,2048,256]{2,1,0:T(8,128)} %get-tuple-element.894, f32[]{:T(128)S(6)} %convert_element_type.121, pred[]{:T(512)S(6)} %compare.9, f32[8,2048,256]{2,1,0:T(8,128)} %get-tuple-element.893), kind=kLoop, calls=%fused_computation.42.clone.1 | loop fusion | flops 25165824 | bytes 100663304 | tf_op jit(solution)/shard_map/while/body/eval_jaxpr/add | solution.py:169
  1780.6 19.9 %psum.22 = f32[128]{0:T(128)S(1)} all-reduce(f32[128]{0:T(128)S(1)} %get-tuple-element.816), channel_id=1, replica_groups=mesh['sweep'=2,'tp'=8,'pp'=2] {'tp'}, use_global_device_ids=true, to_apply=%region_8.9 | all-reduce | flops 128 | bytes 1024 | tf_op jit(solution)/shard_map/while/body/eval_jaxpr/psum | solution.py:124
  1803.6 16.3 select_add_fusion.2
  1830.2 17.8 convert_bitcast_fusion.1
  (302 shorter events, 259.4 us)
Async XLA Ops:
  23.3 740.8 %copy-start.12 = (s32[3]{0:T(128)S(1)}, s32[3]{0:T(128)}, u32[]{:S(2)}) copy-start(s32[3]{0:T(128)} %pad_add_fusion) | copy-start | bytes 40
  23.3 740.8 %copy-start.14 = (s32[3]{0:T(128)S(1)}, s32[3]{0:T(128)}, u32[]{:S(2)}) copy-start(s32[3]{0:T(128)} %iota.11) | copy-start | bytes 40
  48.1 9.2 collective-permute-start.1
  48.2 10.9 collective-permute-start
  243.1 23.0 %collective-permute-start.2 = (f32[128,1024]{0,1:T(8,128)}, f32[128,1024]{0,1:T(8,128)}, u32[]{:S(2)}, u32[]{:S(2)}) collective-permute-start(f32[128,1024]{0,1:T(8,128)} %get-tuple-element.782), channel_id=1, source_target_pairs={{0,14},{2,0},{4,2},{6,4},{8,6},{10,8},{12,10},{14,12},{1,15},{3,1}... | collective-permute-start | bytes 1572872 | tf_op jit(solution)/shard_map/while/body/eval_jaxpr/ppermute | solution.py:19
  245.9 20.1 %collective-permute-start.3 = (f32[128,1024]{0,1:T(8,128)}, f32[128,1024]{0,1:T(8,128)}, u32[]{:S(2)}, u32[]{:S(2)}) collective-permute-start(f32[128,1024]{0,1:T(8,128)} %get-tuple-element.783), channel_id=1, source_target_pairs={{0,2},{2,4},{4,6},{6,8},{8,10},{10,12},{12,14},{14,0},{1,3},{3,5},... | collective-permute-start | bytes 1572872 | tf_op jit(solution)/shard_map/while/body/eval_jaxpr/ppermute | solution.py:19
  268.0 2.9 collective-permute-start.4
  292.7 9.2 collective-permute-start.1
  292.7 11.4 collective-permute-start
  488.1 23.3 %collective-permute-start.2 = (f32[128,1024]{0,1:T(8,128)}, f32[128,1024]{0,1:T(8,128)}, u32[]{:S(2)}, u32[]{:S(2)}) collective-permute-start(f32[128,1024]{0,1:T(8,128)} %get-tuple-element.782), channel_id=1, source_target_pairs={{0,14},{2,0},{4,2},{6,4},{8,6},{10,8},{12,10},{14,12},{1,15},{3,1}... | collective-permute-start | bytes 1572872 | tf_op jit(solution)/shard_map/while/body/eval_jaxpr/ppermute | solution.py:19
  490.5 20.8 %collective-permute-start.3 = (f32[128,1024]{0,1:T(8,128)}, f32[128,1024]{0,1:T(8,128)}, u32[]{:S(2)}, u32[]{:S(2)}) collective-permute-start(f32[128,1024]{0,1:T(8,128)} %get-tuple-element.783), channel_id=1, source_target_pairs={{0,2},{2,4},{4,6},{6,8},{8,10},{10,12},{12,14},{14,0},{1,3},{3,5},... | collective-permute-start | bytes 1572872 | tf_op jit(solution)/shard_map/while/body/eval_jaxpr/ppermute | solution.py:19
  513.3 3.0 collective-permute-start.4
  538.0 9.2 collective-permute-start.1
  538.0 11.0 collective-permute-start
  733.0 23.0 %collective-permute-start.2 = (f32[128,1024]{0,1:T(8,128)}, f32[128,1024]{0,1:T(8,128)}, u32[]{:S(2)}, u32[]{:S(2)}) collective-permute-start(f32[128,1024]{0,1:T(8,128)} %get-tuple-element.782), channel_id=1, source_target_pairs={{0,14},{2,0},{4,2},{6,4},{8,6},{10,8},{12,10},{14,12},{1,15},{3,1}... | collective-permute-start | bytes 1572872 | tf_op jit(solution)/shard_map/while/body/eval_jaxpr/ppermute | solution.py:19
  735.8 20.2 %collective-permute-start.3 = (f32[128,1024]{0,1:T(8,128)}, f32[128,1024]{0,1:T(8,128)}, u32[]{:S(2)}, u32[]{:S(2)}) collective-permute-start(f32[128,1024]{0,1:T(8,128)} %get-tuple-element.783), channel_id=1, source_target_pairs={{0,2},{2,4},{4,6},{6,8},{8,10},{10,12},{12,14},{14,0},{1,3},{3,5},... | collective-permute-start | bytes 1572872 | tf_op jit(solution)/shard_map/while/body/eval_jaxpr/ppermute | solution.py:19
  758.0 2.9 collective-permute-start.4
  766.6 68.4 %collective-permute-start.6 = (bf16[128,1024]{0,1:T(8,128)(2,1)S(1)}, bf16[128,1024]{0,1:T(8,128)(2,1)S(1)}, u32[]{:S(2)}, u32[]{:S(2)}) collective-permute-start(bf16[128,1024]{0,1:T(8,128)(2,1)S(1)} %fusion.102), channel_id=1, source_target_pairs={{0,2},{2,4},{4,6},{6,8},{8,10},{10,12},{12,14},{14,0},{1,3},{3,5},... | collective-permute-start | bytes 786440 | tf_op jit(solution)/shard_map/while/body/eval_jaxpr/ppermute | solution.py:19
  768.4 66.6 %collective-permute-start.5 = (bf16[128,1024]{0,1:T(8,128)(2,1)S(1)}, bf16[128,1024]{0,1:T(8,128)(2,1)}, u32[]{:S(2)}, u32[]{:S(2)}) collective-permute-start(bf16[128,1024]{0,1:T(8,128)(2,1)S(1)} %fusion.102), channel_id=1, source_target_pairs={{0,14},{2,0},{4,2},{6,4},{8,6},{10,8},{12,10},{14,12},{1,15},{3,1}... | collective-permute-start | bytes 786440 | tf_op jit(solution)/shard_map/while/body/eval_jaxpr/ppermute | solution.py:19
  835.1 71.4 %copy-start.1 = (f32[128,8,512]{2,0,1:T(8,128)}, f32[128,8,512]{2,0,1:T(8,128)S(1)}, u32[]{:S(2)}) copy-start(f32[128,8,512]{2,0,1:T(8,128)S(1)} %dynamic-slice_bitcast_fusion.4) | copy-start | bytes 6291460 | tf_op jit(solution)/shard_map/while
  930.3 99.4 %copy-start.3 = (bf16[128,8,256]{2,0,1:T(8,128)(2,1)S(1)}, bf16[128,8,256]{2,0,1:T(8,128)(2,1)}, u32[]{:S(2)}) copy-start(bf16[128,8,256]{2,0,1:T(8,128)(2,1)} %get-tuple-element.811) | copy-start | bytes 1572868 | tf_op jit(solution)/shard_map/while
  1027.6 41.3 %collective-permute-start.7 = (f32[128,1024]{0,1:T(8,128)S(1)}, f32[128,1024]{0,1:T(8,128)S(1)}, u32[]{:S(2)}, u32[]{:S(2)}) collective-permute-start(f32[128,1024]{0,1:T(8,128)S(1)} %get-tuple-element.813), channel_id=1, source_target_pairs={{0,14},{2,0},{4,2},{6,4},{8,6},{10,8},{12,10},{14,12},{1,15},{3,1}... | collective-permute-start | bytes 1572872 | tf_op jit(solution)/shard_map/while/body/eval_jaxpr/ppermute | solution.py:19
  1028.0 40.9 %collective-permute-start.8 = (f32[128,1024]{0,1:T(8,128)S(1)}, f32[128,1024]{0,1:T(8,128)S(1)}, u32[]{:S(2)}, u32[]{:S(2)}) collective-permute-start(f32[128,1024]{0,1:T(8,128)S(1)} %get-tuple-element.814), channel_id=1, source_target_pairs={{0,2},{2,4},{4,6},{6,8},{8,10},{10,12},{12,14},{14,0},{1,3},{3,5},... | collective-permute-start | bytes 1572872 | tf_op jit(solution)/shard_map/while/body/eval_jaxpr/ppermute | solution.py:19
  1047.5 21.3 %copy-start.8 = (f32[1,1024]{1,0:T(1,128)S(1)}, f32[1,1024]{1,0:T(1,128)}, u32[]{:S(2)}) copy-start(f32[1,1024]{1,0:T(1,128)} %copy-done.7) | copy-start | bytes 12292 | tf_op jit(solution)/shard_map/while
  1047.5 21.3 %copy-start.11 = (f32[128]{0:T(128)S(1)}, f32[128]{0:T(128)}, u32[]{:S(2)}) copy-start(f32[128]{0:T(128)} %fusion.99) | copy-start | bytes 1540 | tf_op jit(solution)/shard_map/while
  1092.1 12.9 collective-permute-start.9
  1107.5 68.4 %collective-permute-start.6 = (bf16[128,1024]{0,1:T(8,128)(2,1)S(1)}, bf16[128,1024]{0,1:T(8,128)(2,1)S(1)}, u32[]{:S(2)}, u32[]{:S(2)}) collective-permute-start(bf16[128,1024]{0,1:T(8,128)(2,1)S(1)} %fusion.102), channel_id=1, source_target_pairs={{0,2},{2,4},{4,6},{6,8},{8,10},{10,12},{12,14},{14,0},{1,3},{3,5},... | collective-permute-start | bytes 786440 | tf_op jit(solution)/shard_map/while/body/eval_jaxpr/ppermute | solution.py:19
  1107.6 68.4 %collective-permute-start.5 = (bf16[128,1024]{0,1:T(8,128)(2,1)S(1)}, bf16[128,1024]{0,1:T(8,128)(2,1)}, u32[]{:S(2)}, u32[]{:S(2)}) collective-permute-start(bf16[128,1024]{0,1:T(8,128)(2,1)S(1)} %fusion.102), channel_id=1, source_target_pairs={{0,14},{2,0},{4,2},{6,4},{8,6},{10,8},{12,10},{14,12},{1,15},{3,1}... | collective-permute-start | bytes 786440 | tf_op jit(solution)/shard_map/while/body/eval_jaxpr/ppermute | solution.py:19
  1176.0 71.4 %copy-start.1 = (f32[128,8,512]{2,0,1:T(8,128)}, f32[128,8,512]{2,0,1:T(8,128)S(1)}, u32[]{:S(2)}) copy-start(f32[128,8,512]{2,0,1:T(8,128)S(1)} %dynamic-slice_bitcast_fusion.4) | copy-start | bytes 6291460 | tf_op jit(solution)/shard_map/while
  1271.2 99.4 %copy-start.3 = (bf16[128,8,256]{2,0,1:T(8,128)(2,1)S(1)}, bf16[128,8,256]{2,0,1:T(8,128)(2,1)}, u32[]{:S(2)}) copy-start(bf16[128,8,256]{2,0,1:T(8,128)(2,1)} %get-tuple-element.811) | copy-start | bytes 1572868 | tf_op jit(solution)/shard_map/while
  1368.5 53.4 %collective-permute-start.7 = (f32[128,1024]{0,1:T(8,128)S(1)}, f32[128,1024]{0,1:T(8,128)S(1)}, u32[]{:S(2)}, u32[]{:S(2)}) collective-permute-start(f32[128,1024]{0,1:T(8,128)S(1)} %get-tuple-element.813), channel_id=1, source_target_pairs={{0,14},{2,0},{4,2},{6,4},{8,6},{10,8},{12,10},{14,12},{1,15},{3,1}... | collective-permute-start | bytes 1572872 | tf_op jit(solution)/shard_map/while/body/eval_jaxpr/ppermute | solution.py:19
  1368.5 53.3 %collective-permute-start.8 = (f32[128,1024]{0,1:T(8,128)S(1)}, f32[128,1024]{0,1:T(8,128)S(1)}, u32[]{:S(2)}, u32[]{:S(2)}) collective-permute-start(f32[128,1024]{0,1:T(8,128)S(1)} %get-tuple-element.814), channel_id=1, source_target_pairs={{0,2},{2,4},{4,6},{6,8},{8,10},{10,12},{12,14},{14,0},{1,3},{3,5},... | collective-permute-start | bytes 1572872 | tf_op jit(solution)/shard_map/while/body/eval_jaxpr/ppermute | solution.py:19
  1388.4 33.4 %copy-start.8 = (f32[1,1024]{1,0:T(1,128)S(1)}, f32[1,1024]{1,0:T(1,128)}, u32[]{:S(2)}) copy-start(f32[1,1024]{1,0:T(1,128)} %copy-done.7) | copy-start | bytes 12292 | tf_op jit(solution)/shard_map/while
  1388.4 33.4 %copy-start.11 = (f32[128]{0:T(128)S(1)}, f32[128]{0:T(128)}, u32[]{:S(2)}) copy-start(f32[128]{0:T(128)} %fusion.99) | copy-start | bytes 1540 | tf_op jit(solution)/shard_map/while
  1444.7 17.7 collective-permute-start.9
  1446.0 16.4 copy-start.5
  1446.0 16.4 copy-start.10
  1446.0 16.4 copy-start.13
  1465.0 68.5 %collective-permute-start.6 = (bf16[128,1024]{0,1:T(8,128)(2,1)S(1)}, bf16[128,1024]{0,1:T(8,128)(2,1)S(1)}, u32[]{:S(2)}, u32[]{:S(2)}) collective-permute-start(bf16[128,1024]{0,1:T(8,128)(2,1)S(1)} %fusion.102), channel_id=1, source_target_pairs={{0,2},{2,4},{4,6},{6,8},{8,10},{10,12},{12,14},{14,0},{1,3},{3,5},... | collective-permute-start | bytes 786440 | tf_op jit(solution)/shard_map/while/body/eval_jaxpr/ppermute | solution.py:19
  1465.1 68.5 %collective-permute-start.5 = (bf16[128,1024]{0,1:T(8,128)(2,1)S(1)}, bf16[128,1024]{0,1:T(8,128)(2,1)}, u32[]{:S(2)}, u32[]{:S(2)}) collective-permute-start(bf16[128,1024]{0,1:T(8,128)(2,1)S(1)} %fusion.102), channel_id=1, source_target_pairs={{0,14},{2,0},{4,2},{6,4},{8,6},{10,8},{12,10},{14,12},{1,15},{3,1}... | collective-permute-start | bytes 786440 | tf_op jit(solution)/shard_map/while/body/eval_jaxpr/ppermute | solution.py:19
  1533.5 71.4 %copy-start.1 = (f32[128,8,512]{2,0,1:T(8,128)}, f32[128,8,512]{2,0,1:T(8,128)S(1)}, u32[]{:S(2)}) copy-start(f32[128,8,512]{2,0,1:T(8,128)S(1)} %dynamic-slice_bitcast_fusion.4) | copy-start | bytes 6291460 | tf_op jit(solution)/shard_map/while
  1628.8 99.4 %copy-start.3 = (bf16[128,8,256]{2,0,1:T(8,128)(2,1)S(1)}, bf16[128,8,256]{2,0,1:T(8,128)(2,1)}, u32[]{:S(2)}) copy-start(bf16[128,8,256]{2,0,1:T(8,128)(2,1)} %get-tuple-element.811) | copy-start | bytes 1572868 | tf_op jit(solution)/shard_map/while
  1726.0 53.4 %collective-permute-start.7 = (f32[128,1024]{0,1:T(8,128)S(1)}, f32[128,1024]{0,1:T(8,128)S(1)}, u32[]{:S(2)}, u32[]{:S(2)}) collective-permute-start(f32[128,1024]{0,1:T(8,128)S(1)} %get-tuple-element.813), channel_id=1, source_target_pairs={{0,14},{2,0},{4,2},{6,4},{8,6},{10,8},{12,10},{14,12},{1,15},{3,1}... | collective-permute-start | bytes 1572872 | tf_op jit(solution)/shard_map/while/body/eval_jaxpr/ppermute | solution.py:19
  1726.1 53.3 %collective-permute-start.8 = (f32[128,1024]{0,1:T(8,128)S(1)}, f32[128,1024]{0,1:T(8,128)S(1)}, u32[]{:S(2)}, u32[]{:S(2)}) collective-permute-start(f32[128,1024]{0,1:T(8,128)S(1)} %get-tuple-element.814), channel_id=1, source_target_pairs={{0,2},{2,4},{4,6},{6,8},{8,10},{10,12},{12,14},{14,0},{1,3},{3,5},... | collective-permute-start | bytes 1572872 | tf_op jit(solution)/shard_map/while/body/eval_jaxpr/ppermute | solution.py:19
  1746.0 33.4 %copy-start.8 = (f32[1,1024]{1,0:T(1,128)S(1)}, f32[1,1024]{1,0:T(1,128)}, u32[]{:S(2)}) copy-start(f32[1,1024]{1,0:T(1,128)} %copy-done.7) | copy-start | bytes 12292 | tf_op jit(solution)/shard_map/while
  1746.0 33.4 %copy-start.11 = (f32[128]{0:T(128)S(1)}, f32[128]{0:T(128)}, u32[]{:S(2)}) copy-start(f32[128]{0:T(128)} %fusion.99) | copy-start | bytes 1540 | tf_op jit(solution)/shard_map/while
  1802.3 17.7 collective-permute-start.9
  1803.6 16.4 copy-start.5
  (30 other events, 308.1 us)
where the time goes:
time: 1850 us
  other arithmetic  757 us (41%)
  local copies, waits for them, and re-layouts  614 us (33%)
  matrix products  220 us (12%)
  blocking collectives  123 us (7%)
  waiting for transfers between devices  77.7 us (4%)
  starting transfers between devices  52.7 us (3%)
    scatter-add x6, other arithmetic, spread_band(): jnp.zeros((rows, window_width), jnp.float32).at[:, flat_index]  528 us
    gather x9, local copies, waits for them, and re-layouts, take_band(): jnp.take(window, flat_index, axis=1)  521 us
    add x3, other arithmetic, backward_tick(): up_total + weight_on * up_parts  88.1 us
    ppermute x24, waiting for transfers between devices, from_behind(): lax.ppermute(value, axis, [(i, (i + by) % length) for i in range(length)])  77.7 us
    select_n x6, other arithmetic, take_band(): jnp.take(window, flat_index, axis=1)  69.6 us
    psum x3, blocking collectives, layer_forward(): square_sum = lax.psum(jnp.sum(act_f32 * act_f32, axis=1), 'tp')  63.2 us
    psum x3, blocking collectives, layer_backward(): projection = lax.psum(jnp.sum(scaled * normed_f32, axis=1), 'tp') / D  59.9 us
    dot_general x3, matrix products, layer_backward(): jnp.einsum('thi,thj->hij', take_band(window), both_grads, preferred_eleme...  53.6 us
  transfers between devices with their start and end apart: 30, of which 9 were waited for; matrix products, arithmetic and copies ran while one was open for 21% of the time, Pallas kernels for 0%

commit v1 on v0

v1 whole, which is shorter than its diff:
```python
import functools

import jax
import jax.numpy as jnp
from jax import lax
from jax.experimental import pallas as pl
from jax.experimental.pallas import tpu as pltpu
from jax.sharding import PartitionSpec as P

D = 8192
BLK = 256
T_MB = 128
KB = 8
BAND = 2048
EPSILON = 1e-05
VMEM_LIMIT = 56 * 1024 * 1024
F32 = jnp.float32
BF16 = jnp.bfloat16


def dot(a, b):
    return jnp.dot(a, b, preferred_element_type=F32)


def dot_t(a, b):
    return lax.dot_general(a, b, (((1,), (1,)), ((), ())), preferred_element_type=F32)


def band_of(starts_ref, h):
    return pl.ds(pl.multiple_of(starts_ref[h] * BLK, BLK), BAND)


def fill_normed(normed, act_parts, gain_parts, inverse):
    width = act_parts[0].shape[1]
    for i, (act, gain) in enumerate(zip(act_parts, gain_parts)):
        normed[:, i * width : (i + 1) * width] = (
            act[...].astype(F32) * inverse[...] * gain[...].astype(F32)
        ).astype(BF16)


def emit_parts(total, outs):
    width = outs[0].shape[1]
    for i, out in enumerate(outs):
        out[...] = total[:, i * width : (i + 1) * width].astype(out.dtype)


def stage_kernel(parts, with_forward, with_backward, with_save, starts_ref, *refs):
    refs = list(refs)

    def take(n):
        got = refs[:n]
        del refs[:n]
        return got

    act_parts = take(parts)
    gain_parts = take(parts)
    (inverse,) = take(1)
    grad_parts = take(parts) if with_backward else []
    gate_w, up_w, down_w = take(3)
    forward_outs = take(parts) if with_forward else []
    if with_backward:
        backward_outs = take(parts)
        (projection,) = take(1)
    if with_save:
        hidden_out, gate_out, up_out = take(3)
    (normed,) = take(1)
    if with_forward:
        (forward_total,) = take(1)
    if with_backward:
        grads, backward_total = take(2)

    h = pl.program_id(0)

    @pl.when(h == 0)
    def _():
        fill_normed(normed, act_parts, gain_parts, inverse)
        if with_forward:
            forward_total[...] = jnp.zeros_like(forward_total)
        if with_backward:
            width = grad_parts[0].shape[1]
            for i, grad in enumerate(grad_parts):
                grads[:, i * width : (i + 1) * width] = grad[...]
            backward_total[...] = jnp.zeros_like(backward_total)

    columns = band_of(starts_ref, h)
    band_vals = normed[:, columns]
    gate = dot(band_vals, gate_w[...])
    up = dot(band_vals, up_w[...])
    sig = jax.nn.sigmoid(gate)
    silu = gate * sig
    hidden = (silu * up).astype(BF16)
    if with_forward:
        forward_total[:, columns] += dot(hidden, down_w[...])
    if with_backward:
        grad_hidden = dot_t(grads[:, columns], down_w[...])
        grad_gate = (grad_hidden * up * sig * (1.0 + gate * (1.0 - sig))).astype(BF16)
        grad_up = (grad_hidden * silu).astype(BF16)
        backward_total[:, columns] += dot_t(grad_gate, gate_w[...]) + dot_t(grad_up, up_w[...])
    if with_save:
        hidden_out[...] = hidden
        gate_out[...] = grad_gate
        up_out[...] = grad_up

    @pl.when(h == pl.num_programs(0) - 1)
    def _():
        if with_forward:
            emit_parts(forward_total, forward_outs)
        if with_backward:
            emit_parts(backward_total, backward_outs)
            width = act_parts[0].shape[1]
            products = jnp.zeros((projection.shape[0], 1), F32)
            for i, (act, gain) in enumerate(zip(act_parts, gain_parts)):
                scaled = backward_total[:, i * width : (i + 1) * width] * gain[...].astype(F32)
                products += jnp.sum(
                    scaled * (act[...].astype(F32) * inverse[...]), axis=1, keepdims=True
                )
            projection[...] = products


def whole_spec(array):
    return pl.BlockSpec(array.shape, lambda h, s: (0,) * array.ndim)


def weight_specs():
    return [
        pl.BlockSpec((None, None, BAND, BLK), lambda h, s: (0, h, 0, 0)),
        pl.BlockSpec((None, None, BAND, BLK), lambda h, s: (0, h, 0, 0)),
        pl.BlockSpec((None, None, BLK, BAND), lambda h, s: (0, h, 0, 0)),
    ]


def stage(starts, acts, gains, inverse, grads, weights, with_forward, with_save):
    parts = len(acts)
    reach = parts // 2
    rows, width = acts[0].shape
    hidden_blocks = starts.shape[0]
    with_backward = grads is not None
    ins = list(acts) + list(gains) + [inverse] + (list(grads) if with_backward else [])
    kinds = [F32 if i == reach else BF16 for i in range(parts)]
    shapes = []
    if with_forward:
        shapes += [jax.ShapeDtypeStruct((rows, width), kind) for kind in kinds]
    if with_backward:
        shapes += [jax.ShapeDtypeStruct((rows, width), kind) for kind in kinds]
        shapes += [jax.ShapeDtypeStruct((rows, 1), F32)]
    out_specs = [whole_spec(shape) for shape in shapes]
    if with_save:
        shapes += [jax.ShapeDtypeStruct((rows, hidden_blocks * BLK), BF16)] * 3
        out_specs += [pl.BlockSpec((rows, BLK), lambda h, s: (0, h))] * 3
    scratch = [pltpu.VMEM((rows, parts * width), BF16)]
    if with_forward:
        scratch += [pltpu.VMEM((rows, parts * width), F32)]
    if with_backward:
        scratch += [pltpu.VMEM((rows, parts * width), BF16), pltpu.VMEM((rows, parts * width), F32)]
    products = 2 + (1 if with_forward else 0) + (3 if with_backward else 0)
    return pl.pallas_call(
        functools.partial(stage_kernel, parts, with_forward, with_backward, with_save),
        out_shape=shapes,
        grid_spec=pltpu.PrefetchScalarGridSpec(
            num_scalar_prefetch=1,
            grid=(hidden_blocks,),
            in_specs=[whole_spec(array) for array in ins] + weight_specs(),
            out_specs=out_specs,
            scratch_shapes=scratch,
        ),
        compiler_params=pltpu.CompilerParams(vmem_limit_bytes=VMEM_LIMIT),
        cost_estimate=pl.CostEstimate(
            flops=products * 2 * rows * BAND * BLK * hidden_blocks,
            bytes_accessed=6 * BAND * BLK * hidden_blocks,
            transcendentals=0,
        ),
    )(starts, *ins, *weights)


def weight_kernel(parts, starts_ref, *refs):
    act_parts = refs[:parts]
    gain_parts = refs[parts : 2 * parts]
    inverse = refs[2 * parts]
    grad_parts = refs[2 * parts + 1 : 3 * parts + 1]
    hidden, grad_gate, grad_up = refs[3 * parts + 1 : 3 * parts + 4]
    gate_out, up_out, down_out, normed_t, grads = refs[3 * parts + 4 :]
    h = pl.program_id(0)

    @pl.when(h == 0)
    def _():
        width = act_parts[0].shape[1]
        for i, (act, gain, grad) in enumerate(zip(act_parts, gain_parts, grad_parts)):
            grads[:, i * width : (i + 1) * width] = grad[...]
            normed = (act[...].astype(F32) * inverse[...] * gain[...].astype(F32)).astype(BF16)
            normed_t[i * width : (i + 1) * width, :] = normed.T

    columns = band_of(starts_ref, h)
    band_t = normed_t[columns, :]
    gate_out[...] = dot(band_t, grad_gate[...]).astype(BF16)
    up_out[...] = dot(band_t, grad_up[...]).astype(BF16)
    down_out[...] = dot(hidden[...].T, grads[:, columns]).astype(BF16)


def weight_grads(starts, acts, gains, inverse, grads, saved, weights):
    parts = len(acts)
    rows, width = acts[0].shape
    hidden_blocks = starts.shape[0]
    ins = list(acts) + list(gains) + [inverse] + list(grads)
    return pl.pallas_call(
        functools.partial(weight_kernel, parts),
        out_shape=[jax.ShapeDtypeStruct(w.shape, BF16) for w in weights],
        grid_spec=pltpu.PrefetchScalarGridSpec(
            num_scalar_prefetch=1,
            grid=(hidden_blocks,),
            in_specs=[whole_spec(array) for array in ins]
            + [pl.BlockSpec((rows, BLK), lambda h, s: (0, h))] * 3,
            out_specs=weight_specs(),
            scratch_shapes=[
                pltpu.VMEM((parts * width, rows), BF16),
                pltpu.VMEM((rows, parts * width), BF16),
            ],
        ),
        compiler_params=pltpu.CompilerParams(vmem_limit_bytes=VMEM_LIMIT),
        cost_estimate=pl.CostEstimate(
            flops=6 * rows * BAND * BLK * hidden_blocks,
            bytes_accessed=6 * BAND * BLK * hidden_blocks,
            transcendentals=0,
        ),
    )(starts, *ins, *saved)


def shards(tokens, cotangent, norm_gain, gate_band, up_band, down_band, offsets, counts):
    width = tokens.shape[1]
    blocks_dev = width // BLK
    reach = (KB // 2 - 1 + blocks_dev) // blocks_dev
    section = lax.axis_index("pp")
    position = lax.axis_index("tp")
    count = lax.axis_size("tp")
    sections = lax.axis_size("pp")
    first = section == 0
    starts = jnp.mod(offsets[0] - (position - reach) * blocks_dev, D // BLK)
    weights = (gate_band, up_band, down_band)
    strides = [s for s in range(-reach, reach + 1)]

    def move(value, by, pairs):
        perm = [
            (i * sections + source, (i + by) % count * sections + target)
            for source, target in pairs
            for i in range(count)
        ]
        return lax.ppermute(value, ("tp", "pp"), perm)

    def window(value, pairs):
        return [
            value if s == 0 and pairs[0][0] == pairs[0][1] else move(value, -s, pairs)
            for s in strides
        ]

    def band_sum(pieces, pairs):
        total = pieces[reach]
        for i, s in enumerate(strides):
            if s != 0:
                total = total + move(pieces[i], s, pairs).astype(F32)
        return total

    def choose(a, b):
        return [jnp.where(first, x, y) for x, y in zip(a, b)]

    both = [(0, 0), (1, 1)]
    row_ids = jnp.arange(tokens.shape[0], dtype=jnp.int32)
    valid = row_ids % T_MB < jnp.repeat(counts, T_MB, total_repeat_length=tokens.shape[0])
    cot = jnp.where(valid[:, None], cotangent, jnp.zeros((), BF16))

    own = window(jnp.where(first, tokens, cot), both)
    gains = window(norm_gain, both)
    gain_row = norm_gain.astype(F32)
    tokens_f32 = tokens.astype(F32)
    squares = lax.psum(jnp.sum(tokens_f32 * tokens_f32, axis=1), "tp")
    inverse_0 = lax.rsqrt(squares / D + EPSILON)[:, None]

    pieces = stage(starts, own, gains, inverse_0, None, weights, True, False)
    act_1 = (tokens_f32 + band_sum(pieces, [(0, 0)])).astype(BF16)
    act_1_f32 = act_1.astype(F32)
    squares = lax.psum(
        jnp.where(first, jnp.sum(act_1_f32 * act_1_f32, axis=1), 0.0), ("tp", "pp")
    )
    inverse = jnp.where(first, inverse_0, lax.rsqrt(squares / D + EPSILON)[:, None])
    acts = choose(own, window(act_1, [(0, 1)]))
    layer_in = acts[reach].astype(F32)
    normed = layer_in * inverse

    def input_grad(grad, pieces, projection, pairs):
        scaled = band_sum(pieces, pairs) * gain_row
        return (grad.astype(F32) + inverse * (scaled - normed * (projection / D))).astype(BF16)

    parts = len(strides)
    results = stage(starts, acts, gains, inverse, own, weights, True, False)
    forward_1, backward_1, projection = results[:parts], results[parts : 2 * parts], results[-1]
    projection_1 = lax.psum(projection, "tp")
    grad_1 = input_grad(cot, backward_1, projection_1, [(1, 1)])
    out_1 = (layer_in + band_sum(forward_1, [(1, 1)])).astype(BF16)

    grads = choose(window(grad_1, [(1, 0)]), own)
    results = stage(starts, acts, gains, inverse, grads, weights, False, True)
    backward_0, projection, saved = results[:parts], results[parts], results[parts + 1 :]
    projection_0 = lax.psum(projection, "tp")
    grad_0 = input_grad(grads[reach], backward_0, projection_0, [(0, 0)])
    gate_grads, up_grads, down_grads = weight_grads(
        starts, acts, gains, inverse, grads, saved, weights
    )
    return (
        jnp.where(first, act_1, out_1)[None],
        jnp.where(first, grad_0, grad_1)[None],
        gate_grads,
        up_grads,
        down_grads,
    )


def solution(mesh):
    return jax.shard_map(
        shards,
        mesh=mesh,
        in_specs=(
            P(None, "tp"),
            P(None, "tp"),
            P(("sweep", "pp"), "tp"),
            P(("sweep", "pp"), "tp", None, None),
            P(("sweep", "pp"), "tp", None, None),
            P(("sweep", "pp"), "tp", None, None),
            P(("sweep", "pp"), "tp"),
            P("sweep"),
        ),
        out_specs=(
            P(("sweep", "pp"), None, "tp"),
            P(("sweep", "pp"), None, "tp"),
            P(("sweep", "pp"), "tp", None, None),
            P(("sweep", "pp"), "tp", None, None),
            P(("sweep", "pp"), "tp", None, None),
        ),
        check_vma=False,
    )
```

time: 1850 us -> 320 us (0.17)
  other arithmetic: 757 us -> 19.5 us
  local copies, waits for them, and re-layouts: 614 us -> 4.54 us
  matrix products: 220 us -> 0 us
  Pallas kernels: 0 us -> 94 us
  waiting for transfers between devices: 77.7 us -> 21.7 us
  blocking collectives: 123 us -> 143 us
    scatter-add x6 -> x0, other arithmetic: 528 us -> none  [spread_band(): jnp.zeros((rows, window_width), jnp.float32).at[:, flat_index]]
    gather x9 -> x1, local copies, waits for them, and re-layouts: 521 us -> 1.31 us  [shards(): jnp.repeat(counts, T_MB, total_repeat_length=tokens.shape[0])]
    dot_general x18 -> x0, matrix products: 220 us -> none  [the longest x3 53.6 us: layer_backward(): jnp.einsum('thi,thj->hij', take_band(window), both_grads, preferred_eleme...]
    pallas_call x0 -> x4, Pallas kernels: none -> 94 us  [the longest x3 79 us: stage(): pl.pallas_call(functools.partial(stage_kernel, parts, with_forward, with_...]
    add x3 -> x1, other arithmetic: 88.1 us -> 0.01 us  [shards(): jnp.repeat(counts, T_MB, total_repeat_length=tokens.shape[0])]
    select_n x15 -> x10, other arithmetic: 70.1 us -> 10.9 us  [the longest x6 8.31 us: choose(): return [jnp.where(first, x, y) for x, y in zip(a, b)]]
    ppermute x30 -> x18, waiting for transfers between devices: 77.7 us -> 21.7 us  [move(): return lax.ppermute(value, ('tp', 'pp'), perm)]
    transpose x6 -> x0, local copies, waits for them, and re-layouts: 54.8 us -> none  [the longest x3 27.5 us: layer_backward(): jnp.einsum('thj,hij->thi', both_grads, gate_up_weight, preferred_element_...]
  transfers between devices with their start and end apart: 30 -> 18, of which waited for: 9 -> 2; matrix products, arithmetic and copies ran while one was open for 21% -> 5% of each run, Pallas kernels for 0% -> 14%
where the time goes in v1:
time: 320 us; the launch traced here: 318 us
  blocking collectives  143 us (45%)
  Pallas kernels  94 us (29%)
  starting transfers between devices  34.9 us (11%)
  waiting for transfers between devices  21.7 us (7%)
  other arithmetic  19.5 us (6%)
  local copies, waits for them, and re-layouts  4.54 us (1%)
    pallas_call x3, Pallas kernels, stage(): pl.pallas_call(functools.partial(stage_kernel, parts, with_forward, with_...  79 us
    psum x1, blocking collectives, shards(): projection_0 = lax.psum(projection, 'tp')  43.3 us
    psum x1, blocking collectives, shards(): projection_1 = lax.psum(projection, 'tp')  34.9 us
    ppermute x18, starting transfers between devices, move(): return lax.ppermute(value, ('tp', 'pp'), perm)  34.9 us
    psum x1, blocking collectives, shards(): squares = lax.psum(jnp.sum(tokens_f32 * tokens_f32, axis=1), 'tp')  32.8 us
    psum x1, blocking collectives, shards(): lax.psum(jnp.where(first, jnp.sum(act_1_f32 * act_1_f32, axis=1), 0.0), (...  31.7 us
    ppermute x18, waiting for transfers between devices, move(): return lax.ppermute(value, ('tp', 'pp'), perm)  21.7 us
    pallas_call x1, Pallas kernels, weight_grads(): pl.pallas_call(functools.partial(weight_kernel, parts), out_shape=[jax.Sh...  15.1 us
  transfers between devices with their start and end apart: 18, of which 2 were waited for; matrix products, arithmetic and copies ran while one was open for 5% of the time, Pallas kernels for 14%

profile of v1, /device:TPU:0, one launch (start us, length us, event | category | flops | bytes accessed | tf_op | source)
XLA Modules:
  0.0 318.5 jit_solution(5230342419090940403)
XLA Ops:
  0.6 6.1 %collective-permute-start.3 = (bf16[1,1024]{1,0:T(2,128)(2,1)}, bf16[1,1024]{1,0:T(2,128)(2,1)S(1)}, u32[]{:S(2)}, u32[]{:S(2)}) collective-permute-start(bf16[1,1024]{1,0:T(2,128)(2,1)} %refs_4_.7), channel_id=1, source_target_pairs={{0,14},{2,0},{4,2},{6,4},{8,6},{10,8},{12,10},{14,12},{1,15},{3,1}... | collective-permute-start | bytes 6152 | tf_op jit(solution)/shard_map/ppermute | solution.py:246
  6.7 1.3 fusion.22
  8.0 1.3 compare_select_fusion.1
  9.3 1.3 broadcast_select_fusion.7.refs_1_.refs_8_
  10.7 4.8 %collective-permute-start.1 = (bf16[256,1024]{1,0:T(8,128)(2,1)S(1)}, bf16[256,1024]{1,0:T(8,128)(2,1)S(1)}, u32[]{:S(2)}, u32[]{:S(2)}) collective-permute-start(bf16[256,1024]{1,0:T(8,128)(2,1)S(1)} %broadcast_select_fusion.7.refs_1_.refs_8_), channel_id=1, source_target_pairs={{0,14},{2,0},{4,2},{6,4},{8,6},{10,8},{12,10},{14,12},{1,15},{3,1}... | collective-permute-start | bytes 1572872 | tf_op jit(solution)/shard_map/ppermute | solution.py:246
  15.5 1.2 fusion.10
  16.7 32.8 %psum.28 = f32[256]{0:T(256)S(1)} all-reduce(f32[256]{0:T(256)S(1)} %fusion.10), channel_id=1, replica_groups=mesh['sweep'=2,'tp'=8,'pp'=2] {'tp'}, use_global_device_ids=true, to_apply=%region_1.2 | all-reduce | flops 256 | bytes 2048 | tf_op jit(solution)/shard_map/psum | solution.py:273
  49.5 1.2 and_select_fusion.2.starts_ref
  50.8 0.8 copy.13.refs_6_
  51.6 0.0 copy-start.4
  51.6 0.5 copy-done.16
  52.2 0.2 copy-done.4
  52.4 0.8 copy-done.2
  53.2 17.0 %shard_map.119 = (bf16[256,1024]{1,0:T(8,128)(2,1)}, f32[256,1024]{1,0:T(8,128)}, bf16[256,1024]{1,0:T(8,128)(2,1)}) custom-call(s32[8]{0:T(128)} %and_select_fusion.2.starts_ref, bf16[256,1024]{1,0:T(8,128)(2,1)} %copy-done.2, bf16[256,1024]{1,0:T(8,128)(2,1)} %copy-done, bf16[256,1024]{1,0:T(8,128)(2,1)} %copy-done.4, bf16[1,1024]{1,0:T(2,128)(2,1)} %copy-done.17, ...), custom_call_target="tpu_custom_call" | custom-call | flops 6442450944 | bytes 25165824 | tf_op jit(solution)/shard_map/pallas_call | solution.py:156
  70.2 1.9 collective-permute-start.4
  72.1 3.9 %collective-permute-start.5 = (bf16[256,1024]{1,0:T(8,128)(2,1)}, bf16[256,1024]{1,0:T(8,128)(2,1)S(1)}, u32[]{:S(2)}, u32[]{:S(2)}) collective-permute-start(bf16[256,1024]{1,0:T(8,128)(2,1)} %get-tuple-element.39), channel_id=1, source_target_pairs={{0,2},{2,4},{4,6},{6,8},{8,10},{10,12},{12,14},{14,0},{16,18},{18,... | collective-permute-start | bytes 1572872 | tf_op jit(solution)/shard_map/ppermute | solution.py:246
  76.1 11.0 %collective-permute-done.4 = bf16[256,1024]{1,0:T(8,128)(2,1)S(1)} collective-permute-done((bf16[256,1024]{1,0:T(8,128)(2,1)}, bf16[256,1024]{1,0:T(8,128)(2,1)S(1)}, u32[]{:S(2)}, u32[]{:S(2)}) %collective-permute-start.4) | collective-permute-done | bytes 524320 | tf_op jit(solution)/shard_map/ppermute | solution.py:246
  87.1 1.6 multiply_reduce_fusion
  88.7 1.3 collective-permute-start.8
  90.1 1.3 collective-permute-start.7
  91.4 1.3 collective-permute-start.6
  92.7 31.7 %psum.29 = f32[256]{0:T(256)S(1)} all-reduce(f32[256]{0:T(256)S(1)} %broadcast_select_fusion.8), channel_id=1, replica_groups=mesh['sweep'=2,'tp'=8,'pp'=2] {'tp','pp'}, use_global_device_ids=true, to_apply=%region_3.4 | all-reduce | flops 256 | bytes 2048 | tf_op jit(solution)/shard_map/psum | solution.py:279
  124.5 0.8 copy.14.refs_6_
  125.3 1.9 broadcast_select_fusion.4.refs_2_
  127.2 1.9 broadcast_select_fusion.5.refs_0_
  129.1 1.9 broadcast_select_fusion.6.refs_1_
  131.0 33.1 %shard_map.120 = (bf16[256,1024]{1,0:T(8,128)(2,1)}, f32[256,1024]{1,0:T(8,128)}, bf16[256,1024]{1,0:T(8,128)(2,1)}, bf16[256,1024]{1,0:T(8,128)(2,1)}, f32[256,...) custom-call(s32[8]{0:T(128)} %and_select_fusion.2.starts_ref, ...), custom_call_target="tpu_custom_call" | custom-call | flops 12884901888 | bytes 25165824 | tf_op jit(solution)/shard_map/pallas_call | solution.py:156
  164.2 1.5 collective-permute-start.11
  165.6 1.5 collective-permute-start.12
  167.1 34.9 %psum.30 = f32[256,1]{1,0:T(8,128)S(1)} all-reduce(f32[256,1]{1,0:T(8,128)} %get-tuple-element.46), channel_id=1, replica_groups=mesh['sweep'=2,'tp'=8,'pp'=2] {'tp'}, use_global_device_ids=true, to_apply=%region_4.5 | all-reduce | flops 256 | bytes 2048 | tf_op jit(solution)/shard_map/psum | solution.py:294
  202.0 0.1 multiply_reduce_fusion.2
  202.2 2.0 fusion.5
  204.2 1.3 collective-permute-start.15
  205.5 1.3 collective-permute-start.14
  206.8 0.7 collective-permute-start.9
  207.5 0.7 collective-permute-start.10
  208.2 1.5 collective-permute-start.13
  209.7 10.6 %collective-permute-done.15 = bf16[256,1024]{1,0:T(8,128)(2,1)S(1)} collective-permute-done((bf16[256,1024]{1,0:T(8,128)(2,1)S(1)}, bf16[256,1024]{1,0:T(8,128)(2,1)S(1)}, u32[]{:S(2)}, u32[]{:S(2)}) %collective-permute-start.15) | collective-permute-done | bytes 524320 | tf_op jit(solution)/shard_map/ppermute | solution.py:246
  220.3 0.9 broadcast_select_fusion.1.refs_9_
  221.2 0.9 broadcast_select_fusion.2.refs_7_
  222.1 0.9 broadcast_select_fusion.3.refs_8_
  223.0 28.8 %shard_map.121 = (bf16[256,1024]{1,0:T(8,128)(2,1)}, f32[256,1024]{1,0:T(8,128)}, bf16[256,1024]{1,0:T(8,128)(2,1)}, f32[256,1]{1,0:T(8,128)}, bf16[256,2048]{1,...) custom-call(s32[8]{0:T(128)} %and_select_fusion.2.starts_ref, ...), custom_call_target="tpu_custom_call" | custom-call | flops 10737418240 | bytes 25165824 | tf_op jit(solution)/shard_map/pallas_call | solution.py:156
  251.8 43.3 %psum.31 = f32[256,1]{1,0:T(8,128)S(1)} all-reduce(f32[256,1]{1,0:T(8,128)} %get-tuple-element.50), channel_id=1, replica_groups=mesh['sweep'=2,'tp'=8,'pp'=2] {'tp'}, use_global_device_ids=true, to_apply=%region_5.6 | all-reduce | flops 256 | bytes 2048 | tf_op jit(solution)/shard_map/psum | solution.py:301
  295.1 0.1 multiply_reduce_fusion.1
  295.2 1.9 collective-permute-start.16
  297.1 3.9 %collective-permute-start.17 = (bf16[256,1024]{1,0:T(8,128)(2,1)}, bf16[256,1024]{1,0:T(8,128)(2,1)S(1)}, u32[]{:S(2)}, u32[]{:S(2)}) collective-permute-start(bf16[256,1024]{1,0:T(8,128)(2,1)} %get-tuple-element.49), channel_id=1, source_target_pairs={{0,2},{2,4},{4,6},{6,8},{8,10},{10,12},{12,14},{14,0},{16,18},{18,... | collective-permute-start | bytes 1572872 | tf_op jit(solution)/shard_map/ppermute | solution.py:246
  301.1 15.1 %shard_map.122 = (bf16[1,8,2048,256]{3,2,1,0:T(8,128)(2,1)}, bf16[1,8,2048,256]{3,2,1,0:T(8,128)(2,1)}, bf16[1,8,256,2048]{3,2,1,0:T(8,128)(2,1)}) custom-call(s32[8]{0:T(128)} %and_select_fusion.2.starts_ref, bf16[256,1024]{1,0:T(8,128)(2,1)} %broadcast_select_fusion.5.refs_0_, bf16[256,1024]{1,0:T(8,128)(2,1)} %broadcast_select_fusion.6.refs_1_, ...), custom_call_target="tpu_custom_call" | custom-call | flops 6442450944 | bytes 25165824 | tf_op jit(solution)/shard_map/pallas_call | solution.py:204
  316.2 2.2 fusion.16
  (57 shorter events, 0.2 us)
Async XLA Ops:
  0.6 50.9 %collective-permute-start.3 = (bf16[1,1024]{1,0:T(2,128)(2,1)}, bf16[1,1024]{1,0:T(2,128)(2,1)S(1)}, u32[]{:S(2)}, u32[]{:S(2)}) collective-permute-start(bf16[1,1024]{1,0:T(2,128)(2,1)} %refs_4_.7), channel_id=1, source_target_pairs={{0,14},{2,0},{4,2},{6,4},{8,6},{10,8},{12,10},{14,12},{1,15},{3,1}... | collective-permute-start | bytes 6152 | tf_op jit(solution)/shard_map/ppermute | solution.py:246
  6.7 44.9 %collective-permute-start.2 = (bf16[1,1024]{1,0:T(2,128)(2,1)}, bf16[1,1024]{1,0:T(2,128)(2,1)S(1)}, u32[]{:S(2)}, u32[]{:S(2)}) collective-permute-start(bf16[1,1024]{1,0:T(2,128)(2,1)} %refs_4_.7), channel_id=1, source_target_pairs={{0,2},{2,4},{4,6},{6,8},{8,10},{10,12},{12,14},{14,0},{1,3},{3,5},... | collective-permute-start | bytes 6152 | tf_op jit(solution)/shard_map/ppermute | solution.py:246
  10.7 40.9 %copy-start = (bf16[256,1024]{1,0:T(8,128)(2,1)}, bf16[256,1024]{1,0:T(8,128)(2,1)S(1)}, u32[]{:S(2)}) copy-start(bf16[256,1024]{1,0:T(8,128)(2,1)S(1)} %broadcast_select_fusion.7.refs_1_.refs_8_) | copy-start | bytes 1572868
  10.7 40.9 %collective-permute-start.1 = (bf16[256,1024]{1,0:T(8,128)(2,1)S(1)}, bf16[256,1024]{1,0:T(8,128)(2,1)S(1)}, u32[]{:S(2)}, u32[]{:S(2)}) collective-permute-start(bf16[256,1024]{1,0:T(8,128)(2,1)S(1)} %broadcast_select_fusion.7.refs_1_.refs_8_), channel_id=1, source_target_pairs={{0,14},{2,0},{4,2},{6,4},{8,6},{10,8},{12,10},{14,12},{1,15},{3,1}... | collective-permute-start | bytes 1572872 | tf_op jit(solution)/shard_map/ppermute | solution.py:246
  15.5 36.1 %collective-permute-start = (bf16[256,1024]{1,0:T(8,128)(2,1)S(1)}, bf16[256,1024]{1,0:T(8,128)(2,1)S(1)}, u32[]{:S(2)}, u32[]{:S(2)}) collective-permute-start(bf16[256,1024]{1,0:T(8,128)(2,1)S(1)} %broadcast_select_fusion.7.refs_1_.refs_8_), channel_id=1, source_target_pairs={{0,2},{2,4},{4,6},{6,8},{8,10},{10,12},{12,14},{14,0},{1,3},{3,5},... | collective-permute-start | bytes 1572872 | tf_op jit(solution)/shard_map/ppermute | solution.py:246
  51.6 35.6 %copy-start.6 = (bf16[256,1024]{1,0:T(8,128)(2,1)S(1)}, bf16[256,1024]{1,0:T(8,128)(2,1)}, u32[]{:S(2)}) copy-start(bf16[256,1024]{1,0:T(8,128)(2,1)} %param.10) | copy-start | bytes 1572868
  51.6 0.6 copy-start.16
  51.6 0.6 copy-start.17
  51.6 0.8 copy-start.4
  52.4 0.8 copy-start.2
  70.2 16.9 %collective-permute-start.4 = (bf16[256,1024]{1,0:T(8,128)(2,1)}, bf16[256,1024]{1,0:T(8,128)(2,1)S(1)}, u32[]{:S(2)}, u32[]{:S(2)}) collective-permute-start(bf16[256,1024]{1,0:T(8,128)(2,1)} %get-tuple-element.38), channel_id=1, source_target_pairs={{0,14},{2,0},{4,2},{6,4},{8,6},{10,8},{12,10},{14,12},{16,30},{18,... | collective-permute-start | bytes 1572872 | tf_op jit(solution)/shard_map/ppermute | solution.py:246
  72.1 15.0 %collective-permute-start.5 = (bf16[256,1024]{1,0:T(8,128)(2,1)}, bf16[256,1024]{1,0:T(8,128)(2,1)S(1)}, u32[]{:S(2)}, u32[]{:S(2)}) collective-permute-start(bf16[256,1024]{1,0:T(8,128)(2,1)} %get-tuple-element.39), channel_id=1, source_target_pairs={{0,2},{2,4},{4,6},{6,8},{8,10},{10,12},{12,14},{14,0},{16,18},{18,... | collective-permute-start | bytes 1572872 | tf_op jit(solution)/shard_map/ppermute | solution.py:246
  88.7 36.5 %collective-permute-start.8 = (bf16[256,1024]{1,0:T(8,128)(2,1)S(1)}, bf16[256,1024]{1,0:T(8,128)(2,1)S(1)}, u32[]{:S(2)}, u32[]{:S(2)}) collective-permute-start(bf16[256,1024]{1,0:T(8,128)(2,1)S(1)} %get-tuple-element.58), channel_id=1, source_target_pairs={{0,15},{2,1},{4,3},{6,5},{8,7},{10,9},{12,11},{14,13},{16,31},{18,... | collective-permute-start | bytes 1572872 | tf_op jit(solution)/shard_map/ppermute | solution.py:246
  90.1 37.1 %collective-permute-start.7 = (bf16[256,1024]{1,0:T(8,128)(2,1)S(1)}, bf16[256,1024]{1,0:T(8,128)(2,1)S(1)}, u32[]{:S(2)}, u32[]{:S(2)}) collective-permute-start(bf16[256,1024]{1,0:T(8,128)(2,1)S(1)} %get-tuple-element.58), channel_id=1, source_target_pairs={{0,3},{2,5},{4,7},{6,9},{8,11},{10,13},{12,15},{14,1},{16,19},{18,... | collective-permute-start | bytes 1572872 | tf_op jit(solution)/shard_map/ppermute | solution.py:246
  91.4 37.7 %collective-permute-start.6 = (bf16[256,1024]{1,0:T(8,128)(2,1)S(1)}, bf16[256,1024]{1,0:T(8,128)(2,1)S(1)}, u32[]{:S(2)}, u32[]{:S(2)}) collective-permute-start(bf16[256,1024]{1,0:T(8,128)(2,1)S(1)} %get-tuple-element.58), channel_id=1, source_target_pairs={{0,1},{2,3},{4,5},{6,7},{8,9},{10,11},{12,13},{14,15},{16,17},{18,... | collective-permute-start | bytes 1572872 | tf_op jit(solution)/shard_map/ppermute | solution.py:246
  131.0 36.1 %copy-start.15 = (bf16[1,1024]{1,0:T(2,128)(2,1)S(1)}, bf16[1,1024]{1,0:T(2,128)(2,1)}, u32[]{:S(2)}) copy-start(bf16[1,1024]{1,0:T(2,128)(2,1)} %refs_4_.7) | copy-start | bytes 6148
  131.0 71.2 %copy-start.7 = (bf16[256,1024]{1,0:T(8,128)(2,1)S(1)}, bf16[256,1024]{1,0:T(8,128)(2,1)}, u32[]{:S(2)}) copy-start(bf16[256,1024]{1,0:T(8,128)(2,1)} %broadcast_select_fusion.6.refs_1_) | copy-start | bytes 1572868
  131.0 71.2 %copy-start.9 = (bf16[256,1024]{1,0:T(8,128)(2,1)S(1)}, bf16[256,1024]{1,0:T(8,128)(2,1)}, u32[]{:S(2)}) copy-start(bf16[256,1024]{1,0:T(8,128)(2,1)} %param.11) | copy-start | bytes 1572868
  131.0 89.3 %copy-start.5 = (bf16[256,1024]{1,0:T(8,128)(2,1)S(1)}, bf16[256,1024]{1,0:T(8,128)(2,1)}, u32[]{:S(2)}) copy-start(bf16[256,1024]{1,0:T(8,128)(2,1)} %copy-done.4) | copy-start | bytes 1572868
  131.0 90.2 %copy-start.3 = (bf16[256,1024]{1,0:T(8,128)(2,1)S(1)}, bf16[256,1024]{1,0:T(8,128)(2,1)}, u32[]{:S(2)}) copy-start(bf16[256,1024]{1,0:T(8,128)(2,1)} %copy-done.2) | copy-start | bytes 1572868
  131.0 91.1 %copy-start.1 = (bf16[256,1024]{1,0:T(8,128)(2,1)S(1)}, bf16[256,1024]{1,0:T(8,128)(2,1)}, u32[]{:S(2)}) copy-start(bf16[256,1024]{1,0:T(8,128)(2,1)} %copy-done) | copy-start | bytes 1572868
  164.2 38.0 %collective-permute-start.11 = (bf16[256,1024]{1,0:T(8,128)(2,1)}, bf16[256,1024]{1,0:T(8,128)(2,1)}, u32[]{:S(2)}, u32[]{:S(2)}) collective-permute-start(bf16[256,1024]{1,0:T(8,128)(2,1)} %get-tuple-element.44), channel_id=1, source_target_pairs={{1,15},{3,1},{5,3},{7,5},{9,7},{11,9},{13,11},{15,13},{17,31},{19,... | collective-permute-start | bytes 1572872 | tf_op jit(solution)/shard_map/ppermute | solution.py:246
  165.6 36.5 %collective-permute-start.12 = (bf16[256,1024]{1,0:T(8,128)(2,1)}, bf16[256,1024]{1,0:T(8,128)(2,1)}, u32[]{:S(2)}, u32[]{:S(2)}) collective-permute-start(bf16[256,1024]{1,0:T(8,128)(2,1)} %get-tuple-element.45), channel_id=1, source_target_pairs={{1,3},{3,5},{5,7},{7,9},{9,11},{11,13},{13,15},{15,1},{17,19},{19,... | collective-permute-start | bytes 1572872 | tf_op jit(solution)/shard_map/ppermute | solution.py:246
  204.2 17.9 %copy-start.11 = (bf16[256,1024]{1,0:T(8,128)(2,1)}, bf16[256,1024]{1,0:T(8,128)(2,1)S(1)}, u32[]{:S(2)}) copy-start(bf16[256,1024]{1,0:T(8,128)(2,1)S(1)} %fusion.5) | copy-start | bytes 1572868
  204.2 16.1 %collective-permute-start.15 = (bf16[256,1024]{1,0:T(8,128)(2,1)S(1)}, bf16[256,1024]{1,0:T(8,128)(2,1)S(1)}, u32[]{:S(2)}, u32[]{:S(2)}) collective-permute-start(bf16[256,1024]{1,0:T(8,128)(2,1)S(1)} %fusion.5), channel_id=1, source_target_pairs={{1,14},{3,0},{5,2},{7,4},{9,6},{11,8},{13,10},{15,12},{17,30},{19,... | collective-permute-start | bytes 1572872 | tf_op jit(solution)/shard_map/ppermute | solution.py:246
  205.5 15.7 %collective-permute-start.14 = (bf16[256,1024]{1,0:T(8,128)(2,1)S(1)}, bf16[256,1024]{1,0:T(8,128)(2,1)S(1)}, u32[]{:S(2)}, u32[]{:S(2)}) collective-permute-start(bf16[256,1024]{1,0:T(8,128)(2,1)S(1)} %fusion.5), channel_id=1, source_target_pairs={{1,2},{3,4},{5,6},{7,8},{9,10},{11,12},{13,14},{15,0},{17,18},{19,... | collective-permute-start | bytes 1572872 | tf_op jit(solution)/shard_map/ppermute | solution.py:246
  206.8 109.3 %collective-permute-start.9 = (bf16[256,1024]{1,0:T(8,128)(2,1)}, bf16[256,1024]{1,0:T(8,128)(2,1)S(1)}, u32[]{:S(2)}, u32[]{:S(2)}) collective-permute-start(bf16[256,1024]{1,0:T(8,128)(2,1)} %get-tuple-element.41), channel_id=1, source_target_pairs={{1,15},{3,1},{5,3},{7,5},{9,7},{11,9},{13,11},{15,13},{17,31},{19,... | collective-permute-start | bytes 1572872 | tf_op jit(solution)/shard_map/ppermute | solution.py:246
  207.5 108.6 %collective-permute-start.10 = (bf16[256,1024]{1,0:T(8,128)(2,1)}, bf16[256,1024]{1,0:T(8,128)(2,1)S(1)}, u32[]{:S(2)}, u32[]{:S(2)}) collective-permute-start(bf16[256,1024]{1,0:T(8,128)(2,1)} %get-tuple-element.42), channel_id=1, source_target_pairs={{1,3},{3,5},{5,7},{7,9},{9,11},{11,13},{13,15},{15,1},{17,19},{19,... | collective-permute-start | bytes 1572872 | tf_op jit(solution)/shard_map/ppermute | solution.py:246
  208.2 13.9 %collective-permute-start.13 = (bf16[256,1024]{1,0:T(8,128)(2,1)S(1)}, bf16[256,1024]{1,0:T(8,128)(2,1)S(1)}, u32[]{:S(2)}, u32[]{:S(2)}) collective-permute-start(bf16[256,1024]{1,0:T(8,128)(2,1)S(1)} %fusion.5), channel_id=1, source_target_pairs={{1,0},{3,2},{5,4},{7,6},{9,8},{11,10},{13,12},{15,14},{17,16},{19,... | collective-permute-start | bytes 1572872 | tf_op jit(solution)/shard_map/ppermute | solution.py:246
  295.2 21.0 %collective-permute-start.16 = (bf16[256,1024]{1,0:T(8,128)(2,1)}, bf16[256,1024]{1,0:T(8,128)(2,1)S(1)}, u32[]{:S(2)}, u32[]{:S(2)}) collective-permute-start(bf16[256,1024]{1,0:T(8,128)(2,1)} %get-tuple-element.48), channel_id=1, source_target_pairs={{0,14},{2,0},{4,2},{6,4},{8,6},{10,8},{12,10},{14,12},{16,30},{18,... | collective-permute-start | bytes 1572872 | tf_op jit(solution)/shard_map/ppermute | solution.py:246
  297.1 19.1 %collective-permute-start.17 = (bf16[256,1024]{1,0:T(8,128)(2,1)}, bf16[256,1024]{1,0:T(8,128)(2,1)S(1)}, u32[]{:S(2)}, u32[]{:S(2)}) collective-permute-start(bf16[256,1024]{1,0:T(8,128)(2,1)} %get-tuple-element.49), channel_id=1, source_target_pairs={{0,2},{2,4},{4,6},{6,8},{8,10},{10,12},{12,14},{14,0},{16,18},{18,... | collective-permute-start | bytes 1572872 | tf_op jit(solution)/shard_map/ppermute | solution.py:246
  301.0 15.2 %copy-start.8 = (bf16[256,1024]{1,0:T(8,128)(2,1)S(1)}, bf16[256,1024]{1,0:T(8,128)(2,1)}, u32[]{:S(2)}) copy-start(bf16[256,1024]{1,0:T(8,128)(2,1)} %broadcast_select_fusion.6.refs_1_) | copy-start | bytes 1572868
  301.0 15.2 %copy-start.10 = (bf16[256,1024]{1,0:T(8,128)(2,1)S(1)}, bf16[256,1024]{1,0:T(8,128)(2,1)}, u32[]{:S(2)}) copy-start(bf16[256,1024]{1,0:T(8,128)(2,1)} %broadcast_select_fusion.3.refs_8_) | copy-start | bytes 1572868
  301.1 15.2 %copy-start.12 = (bf16[256,1024]{1,0:T(8,128)(2,1)S(1)}, bf16[256,1024]{1,0:T(8,128)(2,1)}, u32[]{:S(2)}) copy-start(bf16[256,1024]{1,0:T(8,128)(2,1)} %copy-done.11) | copy-start | bytes 1572868
  301.1 15.2 %copy-start.13 = (f32[256,1024]{1,0:T(8,128)S(1)}, f32[256,1024]{1,0:T(8,128)}, u32[]{:S(2)}) copy-start(f32[256,1024]{1,0:T(8,128)} %get-tuple-element.40) | copy-start | bytes 3145732
  301.1 15.2 %copy-start.14 = (f32[256,1024]{1,0:T(8,128)S(1)}, f32[256,1024]{1,0:T(8,128)}, u32[]{:S(2)}) copy-start(f32[256,1024]{1,0:T(8,128)} %get-tuple-element.47) | copy-start | bytes 3145732

commit v2 on v1

--- a/solution.py
+++ b/solution.py
@@ -34,7 +34,7 @@
     width = act_parts[0].shape[1]
     for i, (act, gain) in enumerate(zip(act_parts, gain_parts)):
         normed[:, i * width : (i + 1) * width] = (
-            act[...].astype(F32) * inverse[...] * gain[...].astype(F32)
+            act[...].astype(F32) * inverse[...] * gain[0:1, :]
         ).astype(BF16)
 
 
@@ -110,11 +110,218 @@
             width = act_parts[0].shape[1]
             products = jnp.zeros((projection.shape[0], 1), F32)
             for i, (act, gain) in enumerate(zip(act_parts, gain_parts)):
-                scaled = backward_total[:, i * width : (i + 1) * width] * gain[...].astype(F32)
+                scaled = backward_total[:, i * width : (i + 1) * width] * gain[0:1, :]
                 products += jnp.sum(
                     scaled * (act[...].astype(F32) * inverse[...]), axis=1, keepdims=True
                 )
             projection[...] = products
+
+
+MESH = pl.DeviceIdType.MESH
+
+
+def to_row(column):
+    return jnp.broadcast_to(column, (column.shape[0], 128)).T[0:8, :]
+
+
+def to_column(row):
+    return jnp.broadcast_to(row[0:1, :], (128, row.shape[1])).T[:, 0:1]
+
+
+def place():
+    return lax.axis_index("tp"), lax.axis_index("pp"), lax.axis_size("tp")
+
+
+def shifted(position, by, count):
+    return lax.rem(position + (by % count), count)
+
+
+def greet():
+    position, section, count = place()
+    barrier = pltpu.get_barrier_semaphore()
+    for j in range(count):
+        for other in range(2):
+            if j > 0 or other > 0:
+                pl.semaphore_signal(
+                    barrier,
+                    inc=1,
+                    device_id={
+                        "tp": shifted(position, j, count),
+                        "pp": lax.rem(section + other, 2),
+                    },
+                    device_id_type=MESH,
+                )
+    pl.semaphore_wait(barrier, 2 * count - 1)
+
+
+def copies_to(sources, slots, send, recv, strides, section):
+    position, _, count = place()
+    return [
+        pltpu.make_async_remote_copy(
+            src_ref=source,
+            dst_ref=slots.at[i],
+            send_sem=send.at[i],
+            recv_sem=recv.at[i],
+            device_id={"tp": shifted(position, by, count), "pp": section},
+            device_id_type=MESH,
+        )
+        for i, (source, by) in enumerate(zip(sources, strides))
+    ]
+
+
+def start_all(copies):
+    for copy in copies:
+        copy.start()
+
+
+def others(reach):
+    return [s for s in range(-reach, reach + 1) if s != 0]
+
+
+def first_kernel(reach, mine, tokens, gain, *refs):
+    parts = 2 * reach + 1
+    outs, gain_outs, inverse = refs[:parts], refs[parts : 2 * parts], refs[2 * parts]
+    slots, gain_slots, row, rows, s1, r1, s2, r2, s3, r3 = refs[2 * parts + 1 :]
+    _, section, count = place()
+    strides = [-s for s in others(reach)]
+    greet()
+    moved = copies_to([mine] * len(strides), slots, s1, r1, strides, section)
+    moved_gain = copies_to([gain] * len(strides), gain_slots, s2, r2, strides, section)
+    start_all(moved_gain + moved)
+    act = tokens[...].astype(F32)
+    row[...] = to_row(jnp.sum(act * act, axis=1, keepdims=True))
+    moved_row = copies_to([row] * (count - 1), rows, s3, r3, list(range(1, count)), section)
+    start_all(moved_row)
+    outs[reach][...] = mine[...]
+    gain_outs[reach][...] = gain[...]
+    for copy in moved_row + moved_gain + moved:
+        copy.wait()
+    total = row[...]
+    for j in range(count - 1):
+        total += rows[j]
+    inverse[...] = lax.rsqrt(to_column(total) / D + EPSILON)
+    for i, s in enumerate(others(reach)):
+        outs[reach + s][...] = slots[i]
+        gain_outs[reach + s][...] = gain_slots[i]
+
+
+def act_kernel(reach, *refs):
+    parts = 2 * reach + 1
+    pieces, own, inverse_0 = refs[:parts], refs[parts : 2 * parts], refs[2 * parts]
+    outs, act_1, inverse = refs[2 * parts + 1 : 3 * parts + 1], refs[3 * parts + 1], refs[3 * parts + 2]
+    slots, act_slots, row, rows, s1, r1, s2, r2, s3, r3 = refs[3 * parts + 3 :]
+    _, section, count = place()
+    around = others(reach)
+    greet()
+    moved = copies_to([pieces[reach + s] for s in around], slots, s1, r1, around, section)
+    back = [-s for s in range(-reach, reach + 1)]
+    moved_act = copies_to([act_1] * parts, act_slots, s2, r2, back, 1)
+    moved_row = copies_to([row] * count, rows, s3, r3, list(range(count)), 1)
+
+    @pl.when(section == 0)
+    def _():
+        start_all(moved)
+        for copy in moved:
+            copy.wait()
+        total = pieces[reach][...]
+        for i in range(len(around)):
+            total += slots[i].astype(F32)
+        result = (own[reach][...].astype(F32) + total).astype(BF16)
+        act_1[...] = result
+        start_all(moved_act)
+        wide = result.astype(F32)
+        row[...] = to_row(jnp.sum(wide * wide, axis=1, keepdims=True))
+        start_all(moved_row)
+        inverse[...] = inverse_0[...]
+        for i in range(parts):
+            outs[i][...] = own[i][...]
+        for copy in moved_act + moved_row:
+            copy.wait_send()
+
+    @pl.when(section != 0)
+    def _():
+        act_1[...] = jnp.zeros_like(act_1)
+        for copy in moved_row + moved_act:
+            copy.wait_recv()
+        total = rows[0]
+        for j in range(1, count):
+            total += rows[j]
+        inverse[...] = lax.rsqrt(to_column(total) / D + EPSILON)
+        for i in range(parts):
+            outs[i][...] = act_slots[i]
+
+
+def grad_kernel(reach, source, hand_on, *refs):
+    parts = 2 * reach + 1
+    pieces, own = refs[:parts], refs[parts : 2 * parts]
+    projection, act, gain, inverse = refs[2 * parts : 2 * parts + 4]
+    refs = refs[2 * parts + 4 :]
+    outs = ()
+    if hand_on:
+        outs, refs = refs[:parts], refs[parts:]
+    grad, slots, row, rows, s1, r1, s3, r3 = refs[:8]
+    _, section, count = place()
+    around = others(reach)
+    greet()
+    moved = copies_to([pieces[reach + s] for s in around], slots, s1, r1, around, section)
+    moved_row = copies_to([row] * (count - 1), rows, s3, r3, list(range(1, count)), section)
+    if hand_on:
+        grad_slots, s2, r2 = refs[8:]
+        back = [-s for s in range(-reach, reach + 1)]
+        moved_grad = copies_to([grad] * parts, grad_slots, s2, r2, back, 1 - source)
+
+    @pl.when(section == source)
+    def _():
+        start_all(moved)
+        row[...] = to_row(projection[...])
+        start_all(moved_row)
+        for copy in moved_row + moved:
+            copy.wait()
+        summed = row[...]
+        for j in range(count - 1):
+            summed += rows[j]
+        total = pieces[reach][...]
+        for i in range(len(around)):
+            total += slots[i].astype(F32)
+        scale = inverse[...]
+        normed = act[...].astype(F32) * scale
+        mean = to_column(summed) / D
+        grad[...] = (
+            own[reach][...].astype(F32) + scale * (total * gain[0:1, :] - normed * mean)
+        ).astype(BF16)
+        if hand_on:
+            start_all(moved_grad)
+            for i in range(parts):
+                outs[i][...] = own[i][...]
+            for copy in moved_grad:
+                copy.wait_send()
+
+    @pl.when(section != source)
+    def _():
+        grad[...] = jnp.zeros_like(grad)
+        if hand_on:
+            for copy in moved_grad:
+                copy.wait_recv()
+            for i in range(parts):
+                outs[i][...] = grad_slots[i]
+
+
+def sems(*counts):
+    return [pltpu.SemaphoreType.DMA((n,)) for n in counts for _ in range(2)]
+
+
+def linked(kernel, identity, ins, shapes, scratch):
+    vmem = pl.BlockSpec(memory_space=pltpu.VMEM)
+    return pl.pallas_call(
+        kernel,
+        out_shape=shapes,
+        in_specs=[vmem] * len(ins),
+        out_specs=[vmem] * len(shapes),
+        scratch_shapes=scratch,
+        compiler_params=pltpu.CompilerParams(
+            collective_id=identity, has_side_effects=True, vmem_limit_bytes=VMEM_LIMIT
+        ),
+    )(*ins)
 
 
 def whole_spec(array):
@@ -186,7 +393,7 @@
         width = act_parts[0].shape[1]
         for i, (act, gain, grad) in enumerate(zip(act_parts, gain_parts, grad_parts)):
             grads[:, i * width : (i + 1) * width] = grad[...]
-            normed = (act[...].astype(F32) * inverse[...] * gain[...].astype(F32)).astype(BF16)
+            normed = (act[...].astype(F32) * inverse[...] * gain[0:1, :]).astype(BF16)
             normed_t[i * width : (i + 1) * width, :] = normed.T
 
     columns = band_of(starts_ref, h)
@@ -245,12 +452,6 @@
         ]
         return lax.ppermute(value, ("tp", "pp"), perm)
 
-    def window(value, pairs):
-        return [
-            value if s == 0 and pairs[0][0] == pairs[0][1] else move(value, -s, pairs)
-            for s in strides
-        ]
-
     def band_sum(pieces, pairs):
         total = pieces[reach]
         for i, s in enumerate(strides):
@@ -258,48 +459,70 @@
                 total = total + move(pieces[i], s, pairs).astype(F32)
         return total
 
-    def choose(a, b):
-        return [jnp.where(first, x, y) for x, y in zip(a, b)]
-
-    both = [(0, 0), (1, 1)]
     row_ids = jnp.arange(tokens.shape[0], dtype=jnp.int32)
     valid = row_ids % T_MB < jnp.repeat(counts, T_MB, total_repeat_length=tokens.shape[0])
     cot = jnp.where(valid[:, None], cotangent, jnp.zeros((), BF16))
 
-    own = window(jnp.where(first, tokens, cot), both)
-    gains = window(norm_gain, both)
-    gain_row = norm_gain.astype(F32)
-    tokens_f32 = tokens.astype(F32)
-    squares = lax.psum(jnp.sum(tokens_f32 * tokens_f32, axis=1), "tp")
-    inverse_0 = lax.rsqrt(squares / D + EPSILON)[:, None]
+    rows = tokens.shape[0]
+    parts = len(strides)
+    near = parts - 1
+    block = jax.ShapeDtypeStruct((rows, width), BF16)
+    column = jax.ShapeDtypeStruct((rows, 1), F32)
+    gain = jnp.broadcast_to(norm_gain.astype(F32), (8, width))
+    gain_shape = jax.ShapeDtypeStruct(gain.shape, F32)
+
+    def blocks(n):
+        return pltpu.VMEM((n, rows, width), BF16)
+
+    def stats(n):
+        return [pltpu.VMEM((8, rows), F32), pltpu.VMEM((n, 8, rows), F32)]
+
+    results = linked(
+        functools.partial(first_kernel, reach),
+        0,
+        [jnp.where(first, tokens, cot), tokens, gain],
+        [block] * parts + [gain_shape] * parts + [column],
+        [blocks(near), pltpu.VMEM((near, 8, width), F32)]
+        + stats(count - 1)
+        + sems(near, near, count - 1),
+    )
+    own, gains, inverse_0 = results[:parts], results[parts : 2 * parts], results[-1]
 
     pieces = stage(starts, own, gains, inverse_0, None, weights, True, False)
-    act_1 = (tokens_f32 + band_sum(pieces, [(0, 0)])).astype(BF16)
-    act_1_f32 = act_1.astype(F32)
-    squares = lax.psum(
-        jnp.where(first, jnp.sum(act_1_f32 * act_1_f32, axis=1), 0.0), ("tp", "pp")
-    )
-    inverse = jnp.where(first, inverse_0, lax.rsqrt(squares / D + EPSILON)[:, None])
-    acts = choose(own, window(act_1, [(0, 1)]))
-    layer_in = acts[reach].astype(F32)
-    normed = layer_in * inverse
-
-    def input_grad(grad, pieces, projection, pairs):
-        scaled = band_sum(pieces, pairs) * gain_row
-        return (grad.astype(F32) + inverse * (scaled - normed * (projection / D))).astype(BF16)
-
-    parts = len(strides)
+    results = linked(
+        functools.partial(act_kernel, reach),
+        1,
+        [*pieces, *own, inverse_0],
+        [block] * parts + [block, column],
+        [blocks(near), blocks(parts)] + stats(count) + sems(near, parts, count),
+    )
+    acts, act_1, inverse = results[:parts], results[parts], results[parts + 1]
+
     results = stage(starts, acts, gains, inverse, own, weights, True, False)
     forward_1, backward_1, projection = results[:parts], results[parts : 2 * parts], results[-1]
-    projection_1 = lax.psum(projection, "tp")
-    grad_1 = input_grad(cot, backward_1, projection_1, [(1, 1)])
-    out_1 = (layer_in + band_sum(forward_1, [(1, 1)])).astype(BF16)
-
-    grads = choose(window(grad_1, [(1, 0)]), own)
+    results = linked(
+        functools.partial(grad_kernel, reach, 1, True),
+        2,
+        [*backward_1, *own, projection, acts[reach], gain, inverse],
+        [block] * parts + [block],
+        [blocks(near)]
+        + stats(count - 1)
+        + sems(near, count - 1)
+        + [blocks(parts)]
+        + sems(parts),
+    )
+    grads, grad_1 = results[:parts], results[parts]
+    out_1 = (acts[reach].astype(F32) + band_sum(forward_1, [(1, 1)])).astype(BF16)
+
     results = stage(starts, acts, gains, inverse, grads, weights, False, True)
     backward_0, projection, saved = results[:parts], results[parts], results[parts + 1 :]
-    projection_0 = lax.psum(projection, "tp")
-    grad_0 = input_grad(grads[reach], backward_0, projection_0, [(0, 0)])
+    (grad_0,) = linked(
+        functools.partial(grad_kernel, reach, 0, False),
+        3,
+        [*backward_0, *grads, projection, acts[reach], gain, inverse],
+        [block],
+        [blocks(near)] + stats(count - 1) + sems(near, count - 1),
+    )
     gate_grads, up_grads, down_grads = weight_grads(
         starts, acts, gains, inverse, grads, saved, weights
     )

time: 320 us -> 238 us (0.74)
  blocking collectives: 143 us -> 0 us
  Pallas kernels: 94 us -> 225 us
  starting transfers between devices: 34.9 us -> 1.38 us
  waiting for transfers between devices: 21.7 us -> 0.01 us
  other arithmetic: 19.5 us -> 8.48 us
    psum x4 -> x0, blocking collectives: 143 us -> none  [the longest x1 43.3 us: shards(): projection_0 = lax.psum(projection, 'tp')]
    pallas_call x0 -> x4, Pallas kernels: none -> 132 us  [linked(): pl.pallas_call(kernel, out_shape=shapes, in_specs=[vmem] * len(ins), out_...]
    ppermute x18 -> x2, starting transfers between devices: 34.9 us -> 1.38 us  [move(): return lax.ppermute(value, ('tp', 'pp'), perm)]
    ppermute x18 -> x2, waiting for transfers between devices: 21.7 us -> 0.01 us  [move(): return lax.ppermute(value, ('tp', 'pp'), perm)]
    select_n x9 -> x1, other arithmetic: 9.65 us -> 2.12 us  [shards(): jnp.where(first, tokens, cot)]
  transfers between devices with their start and end apart: 18 -> 2, of which waited for: 2 -> 0; matrix products, arithmetic and copies ran while one was open for 5% -> 1% of each run, Pallas kernels for 14% -> 46%
where the time goes in v2:
time: 238 us
  Pallas kernels  225 us (95%)
  other arithmetic  8.48 us (4%)
    pallas_call x4, Pallas kernels, linked(): pl.pallas_call(kernel, out_shape=shapes, in_specs=[vmem] * len(ins), out_...  132 us
    pallas_call x3, Pallas kernels, stage(): pl.pallas_call(functools.partial(stage_kernel, parts, with_forward, with_...  78.5 us
    pallas_call x1, Pallas kernels, weight_grads(): pl.pallas_call(functools.partial(weight_kernel, parts), out_shape=[jax.Sh...  14.9 us
  transfers between devices with their start and end apart: 2, of which 0 were waited for; matrix products, arithmetic and copies ran while one was open for 1% of the time, Pallas kernels for 46%

profile of v2, /device:TPU:0, one launch (start us, length us, event | category | flops | bytes accessed | tf_op | source)
XLA Modules:
  0.0 237.6 jit_solution(9619755450684346681)
XLA Ops:
  0.7 1.3 fusion.6
  2.0 1.3 compare_select_fusion.1
  3.3 0.7 broadcast_in_dim.45
  4.0 1.2 and_select_fusion.2.starts_ref
  5.2 2.1 select_select_fusion.mine
  7.3 0.6 broadcast_in_dim.42.gain.refs_8_
  7.9 34.7 %shard_map.119 = (bf16[256,1024]{1,0:T(8,128)(2,1)}, bf16[256,1024]{1,0:T(8,128)(2,1)}, bf16[256,1024]{1,0:T(8,128)(2,1)}, f32[8,1024]{1,0:T(8,128)}, f32[8,1024...) custom-call(bf16[256,1024]{1,0:T(8,128)(2,1)} %select_select_fusion.mine, bf16[256,1024]{1,0:T(8,128)(2,1)} %tokens.1, ...), custom_call_target="tpu_custom_call" | custom-call | tf_op jit(solution)/shard_map/pallas_call | solution.py:315
  42.7 17.1 %shard_map.120 = (bf16[256,1024]{1,0:T(8,128)(2,1)}, f32[256,1024]{1,0:T(8,128)}, bf16[256,1024]{1,0:T(8,128)(2,1)}) custom-call(s32[8]{0:T(128)} %and_select_fusion.2.starts_ref, bf16[256,1024]{1,0:T(8,128)(2,1)} %get-tuple-element.53.refs_0_.refs_3_.refs_7_, bf16[256,1024]{1,0:T(8,128)(2,1)} %get-tuple-element.54.refs_1_.refs_4_.refs_8_, ...), custom_call_target="tpu_custom_call" | custom-call | flops 6442450944 | bytes 25165824 | tf_op jit(solution)/shard_map/pallas_call | solution.py:363
  59.7 31.4 %shard_map.121 = (bf16[256,1024]{1,0:T(8,128)(2,1)}, bf16[256,1024]{1,0:T(8,128)(2,1)}, bf16[256,1024]{1,0:T(8,128)(2,1)}, bf16[256,1024]{1,0:T(8,128)(2,1)}, f32[256,1]{1,0:T(8,128)}) custom-call(bf16[256,1024]{1,0:T(8,128)(2,1)} %get-tuple-element.60.refs_0_, f32[256,1024]{1,0:T(8,128)} %get-tuple-element.61.refs_1_, ...), custom_call_target="tpu_custom_call" | custom-call | tf_op jit(solution)/shard_map/pallas_call | solution.py:315
  91.2 32.5 %shard_map.122 = (bf16[256,1024]{1,0:T(8,128)(2,1)}, f32[256,1024]{1,0:T(8,128)}, bf16[256,1024]{1,0:T(8,128)(2,1)}, bf16[256,1024]{1,0:T(8,128)(2,1)}, f32[256,...) custom-call(s32[8]{0:T(128)} %and_select_fusion.2.starts_ref, ...), custom_call_target="tpu_custom_call" | custom-call | flops 12884901888 | bytes 25165824 | tf_op jit(solution)/shard_map/pallas_call | solution.py:363
  123.7 0.7 collective-permute-start
  124.3 0.7 collective-permute-start.1
  125.0 44.1 %shard_map.123 = (bf16[256,1024]{1,0:T(8,128)(2,1)}, bf16[256,1024]{1,0:T(8,128)(2,1)}, bf16[256,1024]{1,0:T(8,128)(2,1)}, bf16[256,1024]{1,0:T(8,128)(2,1)}) custom-call(bf16[256,1024]{1,0:T(8,128)(2,1)} %get-tuple-element.71.refs_0_, f32[256,1024]{1,0:T(8,128)} %get-tuple-element.72.refs_1_, bf16[256,1024]{1,0:T(8,128)(2,1)} %get-tuple-element.73.refs_2_, ...), custom_call_target="tpu_custom_call" | custom-call | tf_op jit(solution)/shard_map/pallas_call | solution.py:315
  169.1 0.0 copy-start.2
  169.1 28.9 %shard_map.124 = (bf16[256,1024]{1,0:T(8,128)(2,1)}, f32[256,1024]{1,0:T(8,128)}, bf16[256,1024]{1,0:T(8,128)(2,1)}, f32[256,1]{1,0:T(8,128)}, bf16[256,2048]{1,...) custom-call(s32[8]{0:T(128)} %and_select_fusion.2.starts_ref, ...), custom_call_target="tpu_custom_call" | custom-call | flops 10737418240 | bytes 25165824 | tf_op jit(solution)/shard_map/pallas_call | solution.py:363
  198.1 21.4 %shard_map.125 = bf16[256,1024]{1,0:T(8,128)(2,1)} custom-call(bf16[256,1024]{1,0:T(8,128)(2,1)} %get-tuple-element.78.refs_0_, f32[256,1024]{1,0:T(8,128)} %get-tuple-element.79.refs_1_, bf16[256,1024]{1,0:T(8,128)(2,1)} %get-tuple-element.80.refs_2_, bf16[256,1024]{1,0:T(8,128)(2,1)} %get-tuple-element.75.refs_7_.refs_3_, ...), custom_call_target="tpu_custom_call" | custom-call | tf_op jit(solution)/shard_map/pallas_call | solution.py:315
  219.5 0.0 copy-done.2
  219.6 1.9 select_bitcast_fusion
  221.5 0.0 copy-start
  221.5 0.0 copy-start.1
  221.5 0.0 copy-start.3
  221.5 14.9 %shard_map.126 = (bf16[1,8,2048,256]{3,2,1,0:T(8,128)(2,1)}, bf16[1,8,2048,256]{3,2,1,0:T(8,128)(2,1)}, bf16[1,8,256,2048]{3,2,1,0:T(8,128)(2,1)}) custom-call(s32[8]{0:T(128)} %and_select_fusion.2.starts_ref, bf16[256,1024]{1,0:T(8,128)(2,1)} %get-tuple-element.65.refs_0_, bf16[256,1024]{1,0:T(8,128)(2,1)} %get-tuple-element.64.refs_1_.refs_7_, ...), custom_call_target="tpu_custom_call" | custom-call | flops 6442450944 | bytes 25165824 | tf_op jit(solution)/shard_map/pallas_call | solution.py:411
  236.3 0.0 collective-permute-done
  236.4 0.0 collective-permute-done.1
  236.4 0.0 copy-done
  236.4 0.0 copy-done.1
  236.4 0.0 copy-done.3
  236.4 1.2 fusion.1
  (3 shorter events, 0.0 us)
Async XLA Ops:
  123.7 112.7 %collective-permute-start = (bf16[256,1024]{1,0:T(8,128)(2,1)}, bf16[256,1024]{1,0:T(8,128)(2,1)S(1)}, u32[]{:S(2)}, u32[]{:S(2)}) collective-permute-start(bf16[256,1024]{1,0:T(8,128)(2,1)} %get-tuple-element.69), channel_id=1, source_target_pairs={{1,15},{3,1},{5,3},{7,5},{9,7},{11,9},{13,11},{15,13},{17,31},{19,... | collective-permute-start | bytes 1572872 | tf_op jit(solution)/shard_map/ppermute | solution.py:453
  124.3 112.0 %collective-permute-start.1 = (bf16[256,1024]{1,0:T(8,128)(2,1)}, bf16[256,1024]{1,0:T(8,128)(2,1)S(1)}, u32[]{:S(2)}, u32[]{:S(2)}) collective-permute-start(bf16[256,1024]{1,0:T(8,128)(2,1)} %get-tuple-element.70), channel_id=1, source_target_pairs={{1,3},{3,5},{5,7},{7,9},{9,11},{11,13},{13,15},{15,1},{17,19},{19,... | collective-permute-start | bytes 1572872 | tf_op jit(solution)/shard_map/ppermute | solution.py:453
  169.1 50.4 %copy-start.2 = (bf16[256,1024]{1,0:T(8,128)(2,1)S(1)}, bf16[256,1024]{1,0:T(8,128)(2,1)}, u32[]{:S(2)}) copy-start(bf16[256,1024]{1,0:T(8,128)(2,1)} %get-tuple-element.82) | copy-start | bytes 1572868
  221.5 14.9 %copy-start = (bf16[256,1024]{1,0:T(8,128)(2,1)S(1)}, bf16[256,1024]{1,0:T(8,128)(2,1)}, u32[]{:S(2)}) copy-start(bf16[256,1024]{1,0:T(8,128)(2,1)} %get-tuple-element.64.refs_1_.refs_7_) | copy-start | bytes 1572868
  221.5 14.9 %copy-start.1 = (f32[256,1024]{1,0:T(8,128)S(1)}, f32[256,1024]{1,0:T(8,128)}, u32[]{:S(2)}) copy-start(f32[256,1024]{1,0:T(8,128)} %get-tuple-element.68) | copy-start | bytes 3145732
  221.5 14.9 %copy-start.3 = (bf16[256,1024]{1,0:T(8,128)(2,1)S(1)}, bf16[256,1024]{1,0:T(8,128)(2,1)}, u32[]{:S(2)}) copy-start(bf16[256,1024]{1,0:T(8,128)(2,1)} %get-tuple-element.63) | copy-start | bytes 1572868

commit v3 on v2

--- a/solution.py
+++ b/solution.py
@@ -178,31 +178,59 @@
     return [s for s in range(-reach, reach + 1) if s != 0]
 
 
-def first_kernel(reach, mine, tokens, gain, *refs):
+def first_kernel(reach, tokens, gain, *refs):
     parts = 2 * reach + 1
     outs, gain_outs, inverse = refs[:parts], refs[parts : 2 * parts], refs[2 * parts]
     slots, gain_slots, row, rows, s1, r1, s2, r2, s3, r3 = refs[2 * parts + 1 :]
     _, section, count = place()
     strides = [-s for s in others(reach)]
     greet()
-    moved = copies_to([mine] * len(strides), slots, s1, r1, strides, section)
+    moved = copies_to([tokens] * len(strides), slots, s1, r1, strides, section)
     moved_gain = copies_to([gain] * len(strides), gain_slots, s2, r2, strides, section)
-    start_all(moved_gain + moved)
-    act = tokens[...].astype(F32)
-    row[...] = to_row(jnp.sum(act * act, axis=1, keepdims=True))
     moved_row = copies_to([row] * (count - 1), rows, s3, r3, list(range(1, count)), section)
-    start_all(moved_row)
-    outs[reach][...] = mine[...]
+    start_all(moved_gain)
+    outs[reach][...] = tokens[...]
     gain_outs[reach][...] = gain[...]
-    for copy in moved_row + moved_gain + moved:
+
+    @pl.when(section == 0)
+    def _():
+        start_all(moved)
+        act = tokens[...].astype(F32)
+        row[...] = to_row(jnp.sum(act * act, axis=1, keepdims=True))
+        start_all(moved_row)
+        for copy in moved_row + moved:
+            copy.wait()
+        total = row[...]
+        for j in range(count - 1):
+            total += rows[j]
+        inverse[...] = lax.rsqrt(to_column(total) / D + EPSILON)
+        for i, s in enumerate(others(reach)):
+            outs[reach + s][...] = slots[i]
+
+    @pl.when(section != 0)
+    def _():
+        inverse[...] = jnp.zeros_like(inverse)
+        for s in others(reach):
+            outs[reach + s][...] = jnp.zeros_like(outs[reach + s])
+
+    for copy in moved_gain:
+        copy.wait()
+    for i, s in enumerate(others(reach)):
+        gain_outs[reach + s][...] = gain_slots[i]
+
+
+def sum_kernel(projection, summed, row, rows, send, recv):
+    _, section, count = place()
+    greet()
+    row[...] = to_row(projection[...])
+    moved = copies_to([row] * (count - 1), rows, send, recv, list(range(1, count)), section)
+    start_all(moved)
+    for copy in moved:
         copy.wait()
     total = row[...]
     for j in range(count - 1):
         total += rows[j]
-    inverse[...] = lax.rsqrt(to_column(total) / D + EPSILON)
-    for i, s in enumerate(others(reach)):
-        outs[reach + s][...] = slots[i]
-        gain_outs[reach + s][...] = gain_slots[i]
+    summed[...] = to_column(total)
 
 
 def act_kernel(reach, *refs):
@@ -480,19 +508,21 @@
     results = linked(
         functools.partial(first_kernel, reach),
         0,
-        [jnp.where(first, tokens, cot), tokens, gain],
+        [tokens, gain],
         [block] * parts + [gain_shape] * parts + [column],
         [blocks(near), pltpu.VMEM((near, 8, width), F32)]
         + stats(count - 1)
         + sems(near, near, count - 1),
     )
-    own, gains, inverse_0 = results[:parts], results[parts : 2 * parts], results[-1]
-
-    pieces = stage(starts, own, gains, inverse_0, None, weights, True, False)
+    acts_0, gains, inverse_0 = results[:parts], results[parts : 2 * parts], results[-1]
+    late_cot, inverse_0 = lax.optimization_barrier((cot, inverse_0))
+    own = [cot if s == 0 else move(late_cot, -s, [(1, 1)]) for s in strides]
+
+    pieces = stage(starts, acts_0, gains, inverse_0, None, weights, True, False)
     results = linked(
         functools.partial(act_kernel, reach),
         1,
-        [*pieces, *own, inverse_0],
+        [*pieces, *acts_0, inverse_0],
         [block] * parts + [block, column],
         [blocks(near), blocks(parts)] + stats(count) + sems(near, parts, count),
     )
@@ -512,17 +542,15 @@
         + sems(parts),
     )
     grads, grad_1 = results[:parts], results[parts]
+    *forward_1, grad_1 = lax.optimization_barrier((*forward_1, grad_1))
     out_1 = (acts[reach].astype(F32) + band_sum(forward_1, [(1, 1)])).astype(BF16)
 
     results = stage(starts, acts, gains, inverse, grads, weights, False, True)
     backward_0, projection, saved = results[:parts], results[parts], results[parts + 1 :]
-    (grad_0,) = linked(
-        functools.partial(grad_kernel, reach, 0, False),
-        3,
-        [*backward_0, *grads, projection, acts[reach], gain, inverse],
-        [block],
-        [blocks(near)] + stats(count - 1) + sems(near, count - 1),
-    )
+    (summed,) = linked(sum_kernel, 3, [projection], [column], stats(count - 1) + sems(count - 1))
+    scaled = band_sum(backward_0, [(0, 0)]) * gain[0:1, :]
+    normed = acts[reach].astype(F32) * inverse
+    grad_0 = (grads[reach].astype(F32) + inverse * (scaled - normed * (summed / D))).astype(BF16)
     gate_grads, up_grads, down_grads = weight_grads(
         starts, acts, gains, inverse, grads, saved, weights
     )

time: 238 us -> 223 us (0.937)
  Pallas kernels: 225 us -> 199 us
  starting transfers between devices: 1.38 us -> 10.9 us
    pallas_call x4, Pallas kernels: 132 us -> 105 us  [linked(): pl.pallas_call(kernel, out_shape=shapes, in_specs=[vmem] * len(ins), out_...]
    ppermute x2 -> x6, starting transfers between devices: 1.38 us -> 10.9 us  [move(): return lax.ppermute(value, ('tp', 'pp'), perm)]
  transfers between devices with their start and end apart: 2 -> 6, of which waited for: 0 -> 0; matrix products, arithmetic and copies ran while one was open for 1% -> 1% of each run, Pallas kernels for 46% -> 49%
where the time goes in v3:
time: 223 us; the launch traced here: 222 us
  Pallas kernels  199 us (89%)
  starting transfers between devices  10.9 us (5%)
  other arithmetic  8.52 us (4%)
  local copies, waits for them, and re-layouts  2.96 us (1%)
    pallas_call x4, Pallas kernels, linked(): pl.pallas_call(kernel, out_shape=shapes, in_specs=[vmem] * len(ins), out_...  105 us
    pallas_call x3, Pallas kernels, stage(): pl.pallas_call(functools.partial(stage_kernel, parts, with_forward, with_...  78.2 us
    pallas_call x1, Pallas kernels, weight_grads(): pl.pallas_call(functools.partial(weight_kernel, parts), out_shape=[jax.Sh...  15.2 us
    ppermute x6, starting transfers between devices, move(): return lax.ppermute(value, ('tp', 'pp'), perm)  10.9 us
  transfers between devices with their start and end apart: 6, of which 0 were waited for; matrix products, arithmetic and copies ran while one was open for 1% of the time, Pallas kernels for 49%

profile of v3, /device:TPU:0, one launch (start us, length us, event | category | flops | bytes accessed | tf_op | source)
XLA Modules:
  0.0 222.0 jit_solution(12876881379386324753)
XLA Ops:
  0.7 1.3 fusion.14
  2.0 1.3 compare_select_fusion.1
  3.3 0.7 broadcast_in_dim.45
  4.0 1.1 broadcast_select_fusion.refs_8_.refs_4_
  5.1 0.0 copy-start
  5.1 0.7 broadcast_in_dim.39.gain.refs_8_
  5.8 23.2 %shard_map.119 = (bf16[256,1024]{1,0:T(8,128)(2,1)}, bf16[256,1024]{1,0:T(8,128)(2,1)}, bf16[256,1024]{1,0:T(8,128)(2,1)}, f32[8,1024]{1,0:T(8,128)}, f32[8,1024...) custom-call(bf16[256,1024]{1,0:T(8,128)(2,1)} %tokens.1, f32[8,1024]{1,0:T(8,128)} %broadcast_in_dim.39.gain.refs_8_), custom_call_target="tpu_custom_call" | custom-call | tf_op jit(solution)/shard_map/pallas_call | solution.py:343
  29.0 0.7 collective-permute-start.1
  29.7 0.7 collective-permute-start
  30.4 1.2 and_select_fusion.2.starts_ref
  31.7 17.0 %shard_map.120 = (bf16[256,1024]{1,0:T(8,128)(2,1)}, f32[256,1024]{1,0:T(8,128)}, bf16[256,1024]{1,0:T(8,128)(2,1)}) custom-call(s32[8]{0:T(128)} %and_select_fusion.2.starts_ref, bf16[256,1024]{1,0:T(8,128)(2,1)} %get-tuple-element.59.refs_0_.refs_3_, bf16[256,1024]{1,0:T(8,128)(2,1)} %get-tuple-element.60.refs_1_.refs_4_, ...), custom_call_target="tpu_custom_call" | custom-call | flops 6442450944 | bytes 25165824 | tf_op jit(solution)/shard_map/pallas_call | solution.py:391
  48.7 0.0 copy-done
  48.7 35.9 %shard_map.121 = (bf16[256,1024]{1,0:T(8,128)(2,1)}, bf16[256,1024]{1,0:T(8,128)(2,1)}, bf16[256,1024]{1,0:T(8,128)(2,1)}, bf16[256,1024]{1,0:T(8,128)(2,1)}, f32[256,1]{1,0:T(8,128)}) custom-call(bf16[256,1024]{1,0:T(8,128)(2,1)} %get-tuple-element.67.refs_0_, f32[256,1024]{1,0:T(8,128)} %get-tuple-element.68.refs_1_, ...), custom_call_target="tpu_custom_call" | custom-call | tf_op jit(solution)/shard_map/pallas_call | solution.py:343
  84.6 1.0 reduce.2
  85.7 0.0 collective-permute-done.1.refs_9_.refs_5_
  85.7 0.0 copy-start.4
  85.7 0.0 collective-permute-done.refs_7_.refs_3_
  85.7 0.0 copy-start.5
  85.7 0.8 copy-done.4
  86.5 0.2 copy-done.5
  86.6 32.4 %shard_map.122 = (bf16[256,1024]{1,0:T(8,128)(2,1)}, f32[256,1024]{1,0:T(8,128)}, bf16[256,1024]{1,0:T(8,128)(2,1)}, bf16[256,1024]{1,0:T(8,128)(2,1)}, f32[256,...) custom-call(s32[8]{0:T(128)} %and_select_fusion.2.starts_ref, ...), custom_call_target="tpu_custom_call" | custom-call | flops 12884901888 | bytes 25165824 | tf_op jit(solution)/shard_map/pallas_call | solution.py:391
  119.0 33.2 %shard_map.123 = (bf16[256,1024]{1,0:T(8,128)(2,1)}, bf16[256,1024]{1,0:T(8,128)(2,1)}, bf16[256,1024]{1,0:T(8,128)(2,1)}, bf16[256,1024]{1,0:T(8,128)(2,1)}) custom-call(bf16[256,1024]{1,0:T(8,128)(2,1)} %get-tuple-element.79.refs_0_, f32[256,1024]{1,0:T(8,128)} %get-tuple-element.80.refs_1_, bf16[256,1024]{1,0:T(8,128)(2,1)} %get-tuple-element.81.refs_2_, ...), custom_call_target="tpu_custom_call" | custom-call | tf_op jit(solution)/shard_map/pallas_call | solution.py:343
  152.2 0.7 collective-permute-start.2
  152.9 0.9 collective-permute-start.3
  153.8 28.8 %shard_map.124 = (bf16[256,1024]{1,0:T(8,128)(2,1)}, f32[256,1024]{1,0:T(8,128)}, bf16[256,1024]{1,0:T(8,128)(2,1)}, f32[256,1]{1,0:T(8,128)}, bf16[256,2048]{1,...) custom-call(s32[8]{0:T(128)} %and_select_fusion.2.starts_ref, ...), custom_call_target="tpu_custom_call" | custom-call | flops 10737418240 | bytes 25165824 | tf_op jit(solution)/shard_map/pallas_call | solution.py:391
  182.6 12.9 %shard_map.125 = f32[256,1]{1,0:T(8,128)} custom-call(f32[256,1]{1,0:T(8,128)} %get-tuple-element.93.projection), custom_call_target="tpu_custom_call" | custom-call | tf_op jit(solution)/shard_map/pallas_call | solution.py:343
  195.5 1.0 multiply_reduce_fusion
  196.5 6.1 %collective-permute-start.4 = (bf16[256,1024]{1,0:T(8,128)(2,1)}, bf16[256,1024]{1,0:T(8,128)(2,1)S(1)}, u32[]{:S(2)}, u32[]{:S(2)}) collective-permute-start(bf16[256,1024]{1,0:T(8,128)(2,1)} %get-tuple-element.91), channel_id=1, source_target_pairs={{0,14},{2,0},{4,2},{6,4},{8,6},{10,8},{12,10},{14,12},{16,30},{18,... | collective-permute-start | bytes 1572872 | tf_op jit(solution)/shard_map/ppermute | solution.py:481
  202.6 1.9 collective-permute-start.5
  204.5 0.0 copy-start.1
  204.5 0.0 copy-start.2
  204.5 0.0 copy-start.3
  204.6 0.0 copy-start.6
  204.6 0.0 copy-start.7
  204.6 0.0 copy-start.8
  204.6 15.2 %shard_map.126 = (bf16[1,8,2048,256]{3,2,1,0:T(8,128)(2,1)}, bf16[1,8,2048,256]{3,2,1,0:T(8,128)(2,1)}, bf16[1,8,256,2048]{3,2,1,0:T(8,128)(2,1)}) custom-call(s32[8]{0:T(128)} %and_select_fusion.2.starts_ref, bf16[256,1024]{1,0:T(8,128)(2,1)} %get-tuple-element.72.refs_0_, bf16[256,1024]{1,0:T(8,128)(2,1)} %get-tuple-element.71.refs_1_.refs_7_, ...), custom_call_target="tpu_custom_call" | custom-call | flops 6442450944 | bytes 25165824 | tf_op jit(solution)/shard_map/pallas_call | solution.py:439
  219.8 0.0 collective-permute-done.2
  219.8 0.0 collective-permute-done.3
  219.8 0.0 collective-permute-done.4
  219.8 0.0 collective-permute-done.5
  219.9 0.0 copy-done.1
  219.9 0.0 copy-done.2
  219.9 0.0 copy-done.3
  219.9 0.0 copy-done.6
  219.9 0.0 copy-done.7
  219.9 0.0 copy-done.8
  219.9 2.1 fusion.9
  (3 shorter events, 0.0 us)
Async XLA Ops:
  5.1 43.6 %copy-start = (bf16[256,1024]{1,0:T(8,128)(2,1)}, bf16[256,1024]{1,0:T(8,128)(2,1)S(1)}, u32[]{:S(2)}) copy-start(bf16[256,1024]{1,0:T(8,128)(2,1)S(1)} %broadcast_select_fusion.refs_8_.refs_4_) | copy-start | bytes 1572868
  29.0 56.6 %collective-permute-start.1 = (bf16[256,1024]{1,0:T(8,128)(2,1)S(1)}, bf16[256,1024]{1,0:T(8,128)(2,1)S(1)}, u32[]{:S(2)}, u32[]{:S(2)}) collective-permute-start(bf16[256,1024]{1,0:T(8,128)(2,1)S(1)} %broadcast_select_fusion.refs_8_.refs_4_), channel_id=1, source_target_pairs={{1,15},{3,1},{5,3},{7,5},{9,7},{11,9},{13,11},{15,13},{17,31},{19,... | collective-permute-start | bytes 1572872 | tf_op jit(solution)/shard_map/ppermute | solution.py:481
  29.7 56.0 %collective-permute-start = (bf16[256,1024]{1,0:T(8,128)(2,1)S(1)}, bf16[256,1024]{1,0:T(8,128)(2,1)S(1)}, u32[]{:S(2)}, u32[]{:S(2)}) collective-permute-start(bf16[256,1024]{1,0:T(8,128)(2,1)S(1)} %broadcast_select_fusion.refs_8_.refs_4_), channel_id=1, source_target_pairs={{1,3},{3,5},{5,7},{7,9},{9,11},{11,13},{13,15},{15,1},{17,19},{19,... | collective-permute-start | bytes 1572872 | tf_op jit(solution)/shard_map/ppermute | solution.py:481
  85.7 0.8 copy-start.4
  85.7 0.9 copy-start.5
  152.2 67.6 %collective-permute-start.2 = (bf16[256,1024]{1,0:T(8,128)(2,1)}, bf16[256,1024]{1,0:T(8,128)(2,1)S(1)}, u32[]{:S(2)}, u32[]{:S(2)}) collective-permute-start(bf16[256,1024]{1,0:T(8,128)(2,1)} %get-tuple-element.85), channel_id=1, source_target_pairs={{1,15},{3,1},{5,3},{7,5},{9,7},{11,9},{13,11},{15,13},{17,31},{19,... | collective-permute-start | bytes 1572872 | tf_op jit(solution)/shard_map/ppermute | solution.py:481
  152.9 66.9 %collective-permute-start.3 = (bf16[256,1024]{1,0:T(8,128)(2,1)}, bf16[256,1024]{1,0:T(8,128)(2,1)S(1)}, u32[]{:S(2)}, u32[]{:S(2)}) collective-permute-start(bf16[256,1024]{1,0:T(8,128)(2,1)} %get-tuple-element.86), channel_id=1, source_target_pairs={{1,3},{3,5},{5,7},{7,9},{9,11},{11,13},{13,15},{15,1},{17,19},{19,... | collective-permute-start | bytes 1572872 | tf_op jit(solution)/shard_map/ppermute | solution.py:481
  196.5 23.3 %collective-permute-start.4 = (bf16[256,1024]{1,0:T(8,128)(2,1)}, bf16[256,1024]{1,0:T(8,128)(2,1)S(1)}, u32[]{:S(2)}, u32[]{:S(2)}) collective-permute-start(bf16[256,1024]{1,0:T(8,128)(2,1)} %get-tuple-element.91), channel_id=1, source_target_pairs={{0,14},{2,0},{4,2},{6,4},{8,6},{10,8},{12,10},{14,12},{16,30},{18,... | collective-permute-start | bytes 1572872 | tf_op jit(solution)/shard_map/ppermute | solution.py:481
  202.6 17.3 %collective-permute-start.5 = (bf16[256,1024]{1,0:T(8,128)(2,1)}, bf16[256,1024]{1,0:T(8,128)(2,1)S(1)}, u32[]{:S(2)}, u32[]{:S(2)}) collective-permute-start(bf16[256,1024]{1,0:T(8,128)(2,1)} %get-tuple-element.92), channel_id=1, source_target_pairs={{0,2},{2,4},{4,6},{6,8},{8,10},{10,12},{12,14},{14,0},{16,18},{18,... | collective-permute-start | bytes 1572872 | tf_op jit(solution)/shard_map/ppermute | solution.py:481
  204.5 15.3 %copy-start.1 = (bf16[256,1024]{1,0:T(8,128)(2,1)S(1)}, bf16[256,1024]{1,0:T(8,128)(2,1)}, u32[]{:S(2)}) copy-start(bf16[256,1024]{1,0:T(8,128)(2,1)} %get-tuple-element.71.refs_1_.refs_7_) | copy-start | bytes 1572868
  204.5 15.3 %copy-start.2 = (f32[256,1024]{1,0:T(8,128)S(1)}, f32[256,1024]{1,0:T(8,128)}, u32[]{:S(2)}) copy-start(f32[256,1024]{1,0:T(8,128)} %get-tuple-element.84) | copy-start | bytes 3145732
  204.5 15.3 %copy-start.3 = (f32[256,1024]{1,0:T(8,128)S(1)}, f32[256,1024]{1,0:T(8,128)}, u32[]{:S(2)}) copy-start(f32[256,1024]{1,0:T(8,128)} %get-tuple-element.90) | copy-start | bytes 3145732
  204.6 15.3 %copy-start.6 = (bf16[256,1024]{1,0:T(8,128)(2,1)S(1)}, bf16[256,1024]{1,0:T(8,128)(2,1)}, u32[]{:S(2)}) copy-start(bf16[256,1024]{1,0:T(8,128)(2,1)} %get-tuple-element.70) | copy-start | bytes 1572868
  204.6 15.3 %copy-start.7 = (bf16[256,1024]{1,0:T(8,128)(2,1)S(1)}, bf16[256,1024]{1,0:T(8,128)(2,1)}, u32[]{:S(2)}) copy-start(bf16[256,1024]{1,0:T(8,128)(2,1)} %get-tuple-element.87.refs_8_) | copy-start | bytes 1572868
  204.6 15.3 %copy-start.8 = (bf16[256,1024]{1,0:T(8,128)(2,1)S(1)}, bf16[256,1024]{1,0:T(8,128)(2,1)}, u32[]{:S(2)}) copy-start(bf16[256,1024]{1,0:T(8,128)(2,1)} %get-tuple-element.94) | copy-start | bytes 1572868

commit v4 on v3

--- a/solution.py
+++ b/solution.py
@@ -136,11 +136,11 @@
     return lax.rem(position + (by % count), count)
 
 
-def greet():
+def greet(sections=2):
     position, section, count = place()
     barrier = pltpu.get_barrier_semaphore()
     for j in range(count):
-        for other in range(2):
+        for other in range(sections):
             if j > 0 or other > 0:
                 pl.semaphore_signal(
                     barrier,
@@ -151,7 +151,7 @@
                     },
                     device_id_type=MESH,
                 )
-    pl.semaphore_wait(barrier, 2 * count - 1)
+    pl.semaphore_wait(barrier, sections * count - 1)
 
 
 def copies_to(sources, slots, send, recv, strides, section):
@@ -184,7 +184,7 @@
     slots, gain_slots, row, rows, s1, r1, s2, r2, s3, r3 = refs[2 * parts + 1 :]
     _, section, count = place()
     strides = [-s for s in others(reach)]
-    greet()
+    greet(1)
     moved = copies_to([tokens] * len(strides), slots, s1, r1, strides, section)
     moved_gain = copies_to([gain] * len(strides), gain_slots, s2, r2, strides, section)
     moved_row = copies_to([row] * (count - 1), rows, s3, r3, list(range(1, count)), section)
@@ -221,7 +221,7 @@
 
 def sum_kernel(projection, summed, row, rows, send, recv):
     _, section, count = place()
-    greet()
+    greet(1)
     row[...] = to_row(projection[...])
     moved = copies_to([row] * (count - 1), rows, send, recv, list(range(1, count)), section)
     start_all(moved)
@@ -547,13 +547,14 @@
 
     results = stage(starts, acts, gains, inverse, grads, weights, False, True)
     backward_0, projection, saved = results[:parts], results[parts], results[parts + 1 :]
+    gate_grads, up_grads, down_grads = weight_grads(
+        starts, acts, gains, inverse, grads, saved, weights
+    )
+    projection, gate_grads = lax.optimization_barrier((projection, gate_grads))
     (summed,) = linked(sum_kernel, 3, [projection], [column], stats(count - 1) + sems(count - 1))
     scaled = band_sum(backward_0, [(0, 0)]) * gain[0:1, :]
     normed = acts[reach].astype(F32) * inverse
     grad_0 = (grads[reach].astype(F32) + inverse * (scaled - normed * (summed / D))).astype(BF16)
-    gate_grads, up_grads, down_grads = weight_grads(
-        starts, acts, gains, inverse, grads, saved, weights
-    )
     return (
         jnp.where(first, act_1, out_1)[None],
         jnp.where(first, grad_0, grad_1)[None],

time: 223 us -> 228 us (1.022)
  Pallas kernels: 199 us -> 204 us
    pallas_call x4, Pallas kernels: 105 us -> 110 us  [linked(): pl.pallas_call(kernel, out_shape=shapes, in_specs=[vmem] * len(ins), out_...]
  transfers between devices with their start and end apart: 6 -> 6, of which waited for: 0 -> 0; matrix products, arithmetic and copies ran while one was open for 1% -> 1% of each run, Pallas kernels for 49% -> 32%
where the time goes in v4:
time: 228 us; the launch traced here: 227 us
  Pallas kernels  204 us (89%)
  starting transfers between devices  11.3 us (5%)
  other arithmetic  8.47 us (4%)
  local copies, waits for them, and re-layouts  2.91 us (1%)
    pallas_call x4, Pallas kernels, linked(): pl.pallas_call(kernel, out_shape=shapes, in_specs=[vmem] * len(ins), out_...  110 us
    pallas_call x3, Pallas kernels, stage(): pl.pallas_call(functools.partial(stage_kernel, parts, with_forward, with_...  78.4 us
    pallas_call x1, Pallas kernels, weight_grads(): pl.pallas_call(functools.partial(weight_kernel, parts), out_shape=[jax.Sh...  15.2 us
    ppermute x6, starting transfers between devices, move(): return lax.ppermute(value, ('tp', 'pp'), perm)  11.3 us
  transfers between devices with their start and end apart: 6, of which 0 were waited for; matrix products, arithmetic and copies ran while one was open for 1% of the time, Pallas kernels for 32%

profile of v4, /device:TPU:0, one launch (start us, length us, event | category | flops | bytes accessed | tf_op | source)
XLA Modules:
  0.0 227.3 jit_solution(16059723533882235443)
XLA Ops:
  0.7 0.7 broadcast_in_dim.45
  1.3 1.3 fusion.14
  2.7 1.3 compare_select_fusion.1
  4.0 0.6 broadcast_in_dim.39.gain.refs_8_
  4.6 33.3 %shard_map.119 = (bf16[256,1024]{1,0:T(8,128)(2,1)}, bf16[256,1024]{1,0:T(8,128)(2,1)}, bf16[256,1024]{1,0:T(8,128)(2,1)}, f32[8,1024]{1,0:T(8,128)}, f32[8,1024...) custom-call(bf16[256,1024]{1,0:T(8,128)(2,1)} %tokens.1, f32[8,1024]{1,0:T(8,128)} %broadcast_in_dim.39.gain.refs_8_), custom_call_target="tpu_custom_call" | custom-call | tf_op jit(solution)/shard_map/pallas_call | solution.py:343
  37.9 1.1 broadcast_select_fusion.refs_8_.refs_4_
  39.1 0.0 copy-start
  39.1 0.7 collective-permute-start
  39.8 0.7 collective-permute-start.1
  40.5 1.2 and_select_fusion.2.starts_ref
  41.7 17.1 %shard_map.120 = (bf16[256,1024]{1,0:T(8,128)(2,1)}, f32[256,1024]{1,0:T(8,128)}, bf16[256,1024]{1,0:T(8,128)(2,1)}) custom-call(s32[8]{0:T(128)} %and_select_fusion.2.starts_ref, bf16[256,1024]{1,0:T(8,128)(2,1)} %get-tuple-element.61.refs_0_.refs_3_, bf16[256,1024]{1,0:T(8,128)(2,1)} %get-tuple-element.62.refs_1_.refs_4_, ...), custom_call_target="tpu_custom_call" | custom-call | flops 6442450944 | bytes 25165824 | tf_op jit(solution)/shard_map/pallas_call | solution.py:391
  58.8 0.0 copy-done
  58.8 32.3 %shard_map.121 = (bf16[256,1024]{1,0:T(8,128)(2,1)}, bf16[256,1024]{1,0:T(8,128)(2,1)}, bf16[256,1024]{1,0:T(8,128)(2,1)}, bf16[256,1024]{1,0:T(8,128)(2,1)}, f32[256,1]{1,0:T(8,128)}) custom-call(bf16[256,1024]{1,0:T(8,128)(2,1)} %get-tuple-element.69.refs_0_, f32[256,1024]{1,0:T(8,128)} %get-tuple-element.70.refs_1_, ...), custom_call_target="tpu_custom_call" | custom-call | tf_op jit(solution)/shard_map/pallas_call | solution.py:343
  91.1 1.0 reduce.2
  92.1 0.0 collective-permute-done.refs_7_.refs_3_
  92.1 0.0 copy-start.4
  92.1 0.0 collective-permute-done.1.refs_9_.refs_5_
  92.2 0.0 copy-start.5
  92.2 0.8 copy-done.4
  92.9 0.2 copy-done.5
  93.1 32.4 %shard_map.122 = (bf16[256,1024]{1,0:T(8,128)(2,1)}, f32[256,1024]{1,0:T(8,128)}, bf16[256,1024]{1,0:T(8,128)(2,1)}, bf16[256,1024]{1,0:T(8,128)(2,1)}, f32[256,...) custom-call(s32[8]{0:T(128)} %and_select_fusion.2.starts_ref, ...), custom_call_target="tpu_custom_call" | custom-call | flops 12884901888 | bytes 25165824 | tf_op jit(solution)/shard_map/pallas_call | solution.py:391
  125.5 36.0 %shard_map.123 = (bf16[256,1024]{1,0:T(8,128)(2,1)}, bf16[256,1024]{1,0:T(8,128)(2,1)}, bf16[256,1024]{1,0:T(8,128)(2,1)}, bf16[256,1024]{1,0:T(8,128)(2,1)}) custom-call(bf16[256,1024]{1,0:T(8,128)(2,1)} %get-tuple-element.81.refs_0_, f32[256,1024]{1,0:T(8,128)} %get-tuple-element.82.refs_1_, bf16[256,1024]{1,0:T(8,128)(2,1)} %get-tuple-element.83.refs_2_, ...), custom_call_target="tpu_custom_call" | custom-call | tf_op jit(solution)/shard_map/pallas_call | solution.py:343
  161.6 0.0 copy-start.10
  161.6 0.0 copy-start.9
  161.6 28.9 %shard_map.124 = (bf16[256,1024]{1,0:T(8,128)(2,1)}, f32[256,1024]{1,0:T(8,128)}, bf16[256,1024]{1,0:T(8,128)(2,1)}, f32[256,1]{1,0:T(8,128)}, bf16[256,2048]{1,...) custom-call(s32[8]{0:T(128)} %and_select_fusion.2.starts_ref, ...), custom_call_target="tpu_custom_call" | custom-call | flops 10737418240 | bytes 25165824 | tf_op jit(solution)/shard_map/pallas_call | solution.py:391
  190.5 3.3 %collective-permute-start.5 = (bf16[256,1024]{1,0:T(8,128)(2,1)}, bf16[256,1024]{1,0:T(8,128)(2,1)S(1)}, u32[]{:S(2)}, u32[]{:S(2)}) collective-permute-start(bf16[256,1024]{1,0:T(8,128)(2,1)} %get-tuple-element.94), channel_id=1, source_target_pairs={{0,2},{2,4},{4,6},{6,8},{8,10},{10,12},{12,14},{14,0},{16,18},{18,... | collective-permute-start | bytes 1572872 | tf_op jit(solution)/shard_map/ppermute | solution.py:481
  193.8 5.3 %collective-permute-start.4 = (bf16[256,1024]{1,0:T(8,128)(2,1)}, bf16[256,1024]{1,0:T(8,128)(2,1)S(1)}, u32[]{:S(2)}, u32[]{:S(2)}) collective-permute-start(bf16[256,1024]{1,0:T(8,128)(2,1)} %get-tuple-element.93), channel_id=1, source_target_pairs={{0,14},{2,0},{4,2},{6,4},{8,6},{10,8},{12,10},{14,12},{16,30},{18,... | collective-permute-start | bytes 1572872 | tf_op jit(solution)/shard_map/ppermute | solution.py:481
  199.0 0.0 copy-done.10
  199.0 0.7 collective-permute-start.3
  199.7 0.0 copy-done.9
  199.8 0.7 collective-permute-start.2
  200.5 0.0 copy-start.1
  200.5 0.0 copy-start.2
  200.5 0.0 copy-start.3
  200.5 15.2 %shard_map.125 = (bf16[1,8,2048,256]{3,2,1,0:T(8,128)(2,1)}, bf16[1,8,2048,256]{3,2,1,0:T(8,128)(2,1)}, bf16[1,8,256,2048]{3,2,1,0:T(8,128)(2,1)}) custom-call(s32[8]{0:T(128)} %and_select_fusion.2.starts_ref, bf16[256,1024]{1,0:T(8,128)(2,1)} %get-tuple-element.74.refs_0_, bf16[256,1024]{1,0:T(8,128)(2,1)} %get-tuple-element.73.refs_1_.refs_7_, ...), custom_call_target="tpu_custom_call" | custom-call | flops 6442450944 | bytes 25165824 | tf_op jit(solution)/shard_map/pallas_call | solution.py:439
  215.8 8.3 %shard_map.126 = f32[256,1]{1,0:T(8,128)} custom-call(f32[256,1]{1,0:T(8,128)} %get-tuple-element.100.projection), custom_call_target="tpu_custom_call" | custom-call | tf_op jit(solution)/shard_map/pallas_call | solution.py:343
  224.1 1.0 multiply_reduce_fusion
  225.1 0.0 collective-permute-done.5
  225.1 0.0 collective-permute-done.4
  225.1 0.0 collective-permute-done.3
  225.1 0.0 collective-permute-done.2
  225.1 0.0 copy-done.1
  225.1 0.0 copy-done.2
  225.1 0.0 copy-done.3
  225.2 0.0 copy-done.6
  225.2 0.0 copy-done.7
  225.2 0.0 copy-done.8
  225.2 2.1 fusion.9
  (6 shorter events, 0.0 us)
Async XLA Ops:
  39.1 19.7 %copy-start = (bf16[256,1024]{1,0:T(8,128)(2,1)}, bf16[256,1024]{1,0:T(8,128)(2,1)S(1)}, u32[]{:S(2)}) copy-start(bf16[256,1024]{1,0:T(8,128)(2,1)S(1)} %broadcast_select_fusion.refs_8_.refs_4_) | copy-start | bytes 1572868
  39.1 53.0 %collective-permute-start = (bf16[256,1024]{1,0:T(8,128)(2,1)S(1)}, bf16[256,1024]{1,0:T(8,128)(2,1)S(1)}, u32[]{:S(2)}, u32[]{:S(2)}) collective-permute-start(bf16[256,1024]{1,0:T(8,128)(2,1)S(1)} %broadcast_select_fusion.refs_8_.refs_4_), channel_id=1, source_target_pairs={{1,3},{3,5},{5,7},{7,9},{9,11},{11,13},{13,15},{15,1},{17,19},{19,... | collective-permute-start | bytes 1572872 | tf_op jit(solution)/shard_map/ppermute | solution.py:481
  39.8 52.3 %collective-permute-start.1 = (bf16[256,1024]{1,0:T(8,128)(2,1)S(1)}, bf16[256,1024]{1,0:T(8,128)(2,1)S(1)}, u32[]{:S(2)}, u32[]{:S(2)}) collective-permute-start(bf16[256,1024]{1,0:T(8,128)(2,1)S(1)} %broadcast_select_fusion.refs_8_.refs_4_), channel_id=1, source_target_pairs={{1,15},{3,1},{5,3},{7,5},{9,7},{11,9},{13,11},{15,13},{17,31},{19,... | collective-permute-start | bytes 1572872 | tf_op jit(solution)/shard_map/ppermute | solution.py:481
  92.1 0.8 copy-start.4
  92.2 0.9 copy-start.5
  161.6 37.5 %copy-start.10 = (bf16[256,1024]{1,0:T(8,128)(2,1)S(1)}, bf16[256,1024]{1,0:T(8,128)(2,1)}, u32[]{:S(2)}) copy-start(bf16[256,1024]{1,0:T(8,128)(2,1)} %get-tuple-element.88) | copy-start | bytes 1572868
  161.6 38.2 %copy-start.9 = (bf16[256,1024]{1,0:T(8,128)(2,1)S(1)}, bf16[256,1024]{1,0:T(8,128)(2,1)}, u32[]{:S(2)}) copy-start(bf16[256,1024]{1,0:T(8,128)(2,1)} %get-tuple-element.87) | copy-start | bytes 1572868
  190.5 34.6 %collective-permute-start.5 = (bf16[256,1024]{1,0:T(8,128)(2,1)}, bf16[256,1024]{1,0:T(8,128)(2,1)S(1)}, u32[]{:S(2)}, u32[]{:S(2)}) collective-permute-start(bf16[256,1024]{1,0:T(8,128)(2,1)} %get-tuple-element.94), channel_id=1, source_target_pairs={{0,2},{2,4},{4,6},{6,8},{8,10},{10,12},{12,14},{14,0},{16,18},{18,... | collective-permute-start | bytes 1572872 | tf_op jit(solution)/shard_map/ppermute | solution.py:481
  193.8 31.3 %collective-permute-start.4 = (bf16[256,1024]{1,0:T(8,128)(2,1)}, bf16[256,1024]{1,0:T(8,128)(2,1)S(1)}, u32[]{:S(2)}, u32[]{:S(2)}) collective-permute-start(bf16[256,1024]{1,0:T(8,128)(2,1)} %get-tuple-element.93), channel_id=1, source_target_pairs={{0,14},{2,0},{4,2},{6,4},{8,6},{10,8},{12,10},{14,12},{16,30},{18,... | collective-permute-start | bytes 1572872 | tf_op jit(solution)/shard_map/ppermute | solution.py:481
  199.0 26.1 %collective-permute-start.3 = (bf16[256,1024]{1,0:T(8,128)(2,1)S(1)}, bf16[256,1024]{1,0:T(8,128)(2,1)S(1)}, u32[]{:S(2)}, u32[]{:S(2)}) collective-permute-start(bf16[256,1024]{1,0:T(8,128)(2,1)S(1)} %copy-done.10), channel_id=1, source_target_pairs={{1,3},{3,5},{5,7},{7,9},{9,11},{11,13},{13,15},{15,1},{17,19},{19,... | collective-permute-start | bytes 1572872 | tf_op jit(solution)/shard_map/ppermute | solution.py:481
  199.8 25.4 %collective-permute-start.2 = (bf16[256,1024]{1,0:T(8,128)(2,1)S(1)}, bf16[256,1024]{1,0:T(8,128)(2,1)S(1)}, u32[]{:S(2)}, u32[]{:S(2)}) collective-permute-start(bf16[256,1024]{1,0:T(8,128)(2,1)S(1)} %copy-done.9), channel_id=1, source_target_pairs={{1,15},{3,1},{5,3},{7,5},{9,7},{11,9},{13,11},{15,13},{17,31},{19,... | collective-permute-start | bytes 1572872 | tf_op jit(solution)/shard_map/ppermute | solution.py:481
  200.5 24.7 %copy-start.1 = (bf16[256,1024]{1,0:T(8,128)(2,1)S(1)}, bf16[256,1024]{1,0:T(8,128)(2,1)}, u32[]{:S(2)}) copy-start(bf16[256,1024]{1,0:T(8,128)(2,1)} %get-tuple-element.73.refs_1_.refs_7_) | copy-start | bytes 1572868
  200.5 24.7 %copy-start.2 = (f32[256,1024]{1,0:T(8,128)S(1)}, f32[256,1024]{1,0:T(8,128)}, u32[]{:S(2)}) copy-start(f32[256,1024]{1,0:T(8,128)} %get-tuple-element.86) | copy-start | bytes 3145732
  200.5 24.7 %copy-start.3 = (f32[256,1024]{1,0:T(8,128)S(1)}, f32[256,1024]{1,0:T(8,128)}, u32[]{:S(2)}) copy-start(f32[256,1024]{1,0:T(8,128)} %get-tuple-element.92) | copy-start | bytes 3145732
  200.5 24.7 %copy-start.6 = (bf16[256,1024]{1,0:T(8,128)(2,1)S(1)}, bf16[256,1024]{1,0:T(8,128)(2,1)}, u32[]{:S(2)}) copy-start(bf16[256,1024]{1,0:T(8,128)(2,1)} %get-tuple-element.72) | copy-start | bytes 1572868
  200.5 24.7 %copy-start.7 = (bf16[256,1024]{1,0:T(8,128)(2,1)S(1)}, bf16[256,1024]{1,0:T(8,128)(2,1)}, u32[]{:S(2)}) copy-start(bf16[256,1024]{1,0:T(8,128)(2,1)} %get-tuple-element.89.refs_8_) | copy-start | bytes 1572868
  200.5 24.7 %copy-start.8 = (bf16[256,1024]{1,0:T(8,128)(2,1)S(1)}, bf16[256,1024]{1,0:T(8,128)(2,1)}, u32[]{:S(2)}) copy-start(bf16[256,1024]{1,0:T(8,128)(2,1)} %get-tuple-element.101) | copy-start | bytes 1572868
